TPU v7x, 512 devices: a whole 4x4x16 slice. The times are simulated.
512 devices in a mesh: ctx: 16 (over z_hi, x, core), head: 32 (over y, z_lo).
Axes of the slice: x: 4, y: 4, z: 16 (z_hi: 2, z_lo: 8; z = z_hi * 8 + z_lo), core: 2. Of those that a mesh axis runs over, the one named last changes fastest.
Arguments:
- query_rows: bfloat16 [32768, 4096], P('ctx', 'head'), may hold values from -6 to 6
- key_rows: bfloat16 [32768, 512], P(('ctx', 'head')), may hold values from -4 to 4
- value_rows: bfloat16 [32768, 512], P(('ctx', 'head')), may hold values from -6 to 6
- selection: int32 [16, 3], replicated, may hold values from -1 to 15, as said below
Outputs:
- attended: bfloat16 [32768, 4096], P('ctx', 'head')
Inputs may be any that keep to these rules, and one draw needn't show every extreme that they name: `selection`: row b names block b first, then up to two different earlier blocks; -1 fills a slot that has no earlier block to name, which happens only in rows 0 and 1.
All inputs are finite; a program needn't handle non-finite values.
Results may differ from a plain program's by a relative error of at most 0.0044.
Values may be sent and summed in bfloat16 or wider, within the bound.
A program may use at most 64 MiB of HBM per device.

v0:
```python
import jax
import jax.numpy as jnp
from jax import lax
from jax.sharding import PartitionSpec as P

HK = 4
DH = 128
BLOCK = 2048


def block_terms(query_head, key_block, value_block, causal):
    length = key_block.shape[0]
    tile = min(512, query_head.shape[0])
    count = query_head.shape[0] // tile
    tiles = query_head.reshape(count, tile, query_head.shape[1])
    scale = query_head.shape[1] ** (-0.5)

    def one_tile(packed):
        rows_q, offset = packed
        scores = (
            lax.dot_general(
                rows_q, key_block, (((1,), (1,)), ((), ())), preferred_element_type=jnp.float32
            )
            * scale
        )
        if causal:
            row_ids = offset + jnp.arange(tile, dtype=jnp.int32)[:, None]
            col_ids = jnp.arange(length, dtype=jnp.int32)[None, :]
            scores = jnp.where(col_ids <= row_ids, scores, -1e30)
        peak = jnp.max(scores, axis=1)
        expos = jnp.exp(scores - peak[:, None])
        mass = jnp.sum(expos, axis=1)
        summed = jnp.dot(
            expos.astype(jnp.bfloat16), value_block, preferred_element_type=jnp.float32
        )
        return (peak, mass, summed)

    peak, mass, summed = lax.map(one_tile, (tiles, jnp.arange(count, dtype=jnp.int32) * tile))
    return (peak.reshape(-1), mass.reshape(-1), summed.reshape(-1, summed.shape[-1]))


def on_device(query_rows, key_rows, value_rows, selection):
    heads_here = query_rows.shape[1] // DH
    siblings = lax.axis_size("head") // HK
    local_tokens = key_rows.shape[0]
    spread_keys = jnp.broadcast_to(
        key_rows.reshape(local_tokens, HK, 1, DH), (local_tokens, HK, siblings, DH)
    ).reshape(local_tokens, HK * siblings * DH)
    spread_values = jnp.broadcast_to(
        value_rows.reshape(local_tokens, HK, 1, DH), (local_tokens, HK, siblings, DH)
    ).reshape(local_tokens, HK * siblings * DH)
    key_local, value_local = (
        lax.all_to_all(spread_keys, "head", split_axis=1, concat_axis=0, tiled=True),
        lax.all_to_all(spread_values, "head", split_axis=1, concat_axis=0, tiled=True),
    )
    group_tokens = key_local.shape[0]
    blocks_here = group_tokens // BLOCK
    queries = query_rows.reshape(blocks_here, BLOCK, heads_here, DH).transpose(0, 2, 1, 3)
    ctx_pos = lax.axis_index("ctx")
    chosen = lax.dynamic_slice_in_dim(selection, ctx_pos * blocks_here, blocks_here, 0)
    state = (
        jnp.full((blocks_here, heads_here, BLOCK), -1e30, jnp.float32),
        jnp.zeros((blocks_here, heads_here, BLOCK), jnp.float32),
        jnp.zeros((blocks_here, heads_here, BLOCK, DH), jnp.float32),
    )

    def absorb(state, query_pos, mode, key_block, value_block):
        peaks, masses, sums = state
        old_peak = peaks[query_pos]
        old_mass = masses[query_pos]
        old_sum = sums[query_pos]

        def keep():
            return (old_peak, old_mass, old_sum)

        def joined(causal):

            def run():
                new_peak, new_mass, new_sum = lax.map(
                    lambda head_rows: block_terms(head_rows, key_block, value_block, causal),
                    queries[query_pos],
                )
                top = jnp.maximum(old_peak, new_peak)
                before = jnp.exp(old_peak - top)
                after = jnp.exp(new_peak - top)
                return (
                    top,
                    old_mass * before + new_mass * after,
                    old_sum * before[..., None] + new_sum * after[..., None],
                )

            return run

        top, mass, summed = lax.switch(mode.astype(jnp.int32), [keep, joined(False), joined(True)])
        return (
            peaks.at[query_pos].set(top),
            masses.at[query_pos].set(mass),
            sums.at[query_pos].set(summed),
        )

    def fold_step(state, pieces):
        key_piece, value_piece = pieces

        def over(block_pos, state):
            key_block = lax.dynamic_slice_in_dim(key_piece, block_pos * BLOCK, BLOCK, 0)
            value_block = lax.dynamic_slice_in_dim(value_piece, block_pos * BLOCK, BLOCK, 0)
            listed = chosen[0]
            mode = jnp.where(
                listed[0] == block_pos,
                2,
                jnp.where((listed[1] == block_pos) | (listed[2] == block_pos), 1, 0),
            )
            state = absorb(state, 0, mode, key_block, value_block)
            return state

        return lax.fori_loop(0, key_piece.shape[0] // BLOCK, over, state)

    state = fold_step(
        state,
        (
            lax.all_gather(key_local, "ctx", axis=0, tiled=True),
            lax.all_gather(value_local, "ctx", axis=0, tiled=True),
        ),
    )
    peaks, masses, sums = state
    output = sums / masses[..., None]
    return output.transpose(0, 2, 1, 3).reshape(group_tokens, heads_here * DH).astype(jnp.bfloat16)


def solution(mesh):
    placed = (P("ctx", "head"), P(("ctx", "head"), None), P(("ctx", "head"), None), P())
    return jax.shard_map(
        on_device, mesh=mesh, in_specs=placed, out_specs=P("ctx", "head"), check_vma=False
    )
```

profile of v0, /device:TPU:3, one launch (start us, length us, event | category | flops | bytes accessed | tf_op | source)
XLA Modules:
  0.0 517.5 jit_solution(8083536835352054935)
XLA Ops:
  6.5 0.8 copy-done
  7.5 44.5 %all_to_all.38 = bf16[64,32,128]{2,0,1:T(8,128)(2,1)} all-to-all(bf16[64,32,128]{2,0,1:T(8,128)(2,1)S(1)} %bitcast.153), channel_id=1, replica_groups=mesh['ctx'=16,'head'=32] {'head'}, dimensions={1} | all-to-all | bytes 1048576 | tf_op jit(solution)/shard_map/all_to_all | solution.py:53
  52.1 0.9 copy_bitcast_fusion
  53.0 55.0 %all_to_all.39 = bf16[64,32,128]{2,0,1:T(8,128)(2,1)} all-to-all(bf16[64,32,128]{2,0,1:T(8,128)(2,1)S(1)} %bitcast.154), channel_id=1, replica_groups=mesh['ctx'=16,'head'=32] {'head'}, dimensions={1} | all-to-all | bytes 1048576 | tf_op jit(solution)/shard_map/all_to_all | solution.py:54
  108.2 132.2 %all-gather.3.cloned.1.call-done = bf16[32768,128]{1,0:T(8,128)(2,1)} async-done(((bf16[2048,128]{1,0:T(8,128)(2,1)}), bf16[32768,128]{1,0:T(8,128)(2,1)}) %all-gather.3.cloned.1.call-update) | async-done | bytes 8388624 | tf_op jit(solution)/shard_map/all_gather | solution.py:121
  240.5 173.8 %all-gather.5.cloned.1.call-done = bf16[32768,128]{1,0:T(8,128)(2,1)} async-done(((bf16[2048,128]{1,0:T(8,128)(2,1)}), bf16[32768,128]{1,0:T(8,128)(2,1)}) %all-gather.5.cloned.1.call-update) | async-done | bytes 8388624 | tf_op jit(solution)/shard_map/all_gather | solution.py:122
  414.4 95.1 %while.105 = (s32[]{:T(128)}, f32[1,1,2048]{2,1,0:T(1,128)S(1)}, f32[1,1,2048]{2,1,0:T(1,128)S(1)}, f32[1,1,2048,128]{3,2,1,0:T(8,128)S(1)}, s32[1,3]{1,0:T(1,12...) while((s32[]{:T(128)}, f32[1,1,2048]{2,1,0:T(1,128)S(1)}, ...), condition=%wide.region_12.13_spmd, body=%wide.region_0.12_spmd.sunk | while | flops 546057728 | bytes 19403912 | solution.py:116
  419.6 16.2 %conditional.2 = (f32[1,1,2048]{2,1,0:T(1,128)S(1)}, f32[1,1,2048]{2,1,0:T(1,128)S(1)}, f32[1,1,2048,128]{3,2,1,0:T(8,128)S(1)}) conditional(s32[]{:T(128)} %clamp.12, (f32[1,2048]{1,0:T(1,128)S(1)}, f32[1,2048]{1,0:T(1,128)S(1)}, f32[1,2048,128]{2,1,0:T(8,128)S(1)}) %tuple.208, (bf16[2048,128]{1,0:T(8,128)(2,1)}, ...), branch_computations={%region_1.1_spmd, %region_2.6_spmd.clone, %region_7.0_spmd.clone} | conditional | flops 546057728 | bytes 19403572 | solution.py:94
  419.6 1.3 constant_dynamic-slice_fusion
  420.9 13.9 %while.103 = (s32[]{:T(128)}, f32[4,512]{1,0:T(4,128)S(1)}, f32[4,512]{1,0:T(4,128)S(1)}, f32[4,512,128]{2,1,0:T(8,128)S(1)}, bf16[4,512,128]{2,1,0:T(8,128)(2,1...) while((s32[]{:T(128)}, f32[4,512]{1,0:T(4,128)S(1)}, ...), condition=%wide.region_6.5_spmd, body=%wide.region_3.4_spmd.sunk | while | flops 545258496 | bytes 14041705 | solution.py:38
  420.9 1.7 multiply_reduce_fusion.2
  422.6 0.9 fusion.67
  423.4 0.8 fusion.66
  424.4 1.7 multiply_reduce_fusion.2
  426.1 0.9 fusion.67
  426.9 0.8 fusion.66
  427.9 1.7 multiply_reduce_fusion.2
  429.6 0.8 fusion.67
  430.4 0.8 fusion.66
  431.3 1.7 multiply_reduce_fusion.2
  433.0 0.9 fusion.67
  433.9 0.8 fusion.66
  434.9 0.9 fusion.32
  438.4 16.2 %conditional.2 = (f32[1,1,2048]{2,1,0:T(1,128)S(1)}, f32[1,1,2048]{2,1,0:T(1,128)S(1)}, f32[1,1,2048,128]{3,2,1,0:T(8,128)S(1)}) conditional(s32[]{:T(128)} %clamp.12, (f32[1,2048]{1,0:T(1,128)S(1)}, f32[1,2048]{1,0:T(1,128)S(1)}, f32[1,2048,128]{2,1,0:T(8,128)S(1)}) %tuple.208, (bf16[2048,128]{1,0:T(8,128)(2,1)}, ...), branch_computations={%region_1.1_spmd, %region_2.6_spmd.clone, %region_7.0_spmd.clone} | conditional | flops 546057728 | bytes 19403572 | solution.py:94
  438.4 1.3 constant_dynamic-slice_fusion
  439.7 13.9 %while.103 = (s32[]{:T(128)}, f32[4,512]{1,0:T(4,128)S(1)}, f32[4,512]{1,0:T(4,128)S(1)}, f32[4,512,128]{2,1,0:T(8,128)S(1)}, bf16[4,512,128]{2,1,0:T(8,128)(2,1...) while((s32[]{:T(128)}, f32[4,512]{1,0:T(4,128)S(1)}, ...), condition=%wide.region_6.5_spmd, body=%wide.region_3.4_spmd.sunk | while | flops 545258496 | bytes 14041705 | solution.py:38
  439.7 1.7 multiply_reduce_fusion.2
  441.4 0.9 fusion.67
  442.3 0.8 fusion.66
  443.2 1.7 multiply_reduce_fusion.2
  444.9 0.9 fusion.67
  445.7 0.8 fusion.66
  446.7 1.7 multiply_reduce_fusion.2
  448.4 0.9 fusion.67
  449.2 0.8 fusion.66
  450.2 1.7 multiply_reduce_fusion.2
  451.9 0.8 fusion.67
  452.7 0.8 fusion.66
  453.7 0.9 fusion.32
  457.2 21.2 %conditional.2 = (f32[1,1,2048]{2,1,0:T(1,128)S(1)}, f32[1,1,2048]{2,1,0:T(1,128)S(1)}, f32[1,1,2048,128]{3,2,1,0:T(8,128)S(1)}) conditional(s32[]{:T(128)} %clamp.12, (f32[1,2048]{1,0:T(1,128)S(1)}, f32[1,2048]{1,0:T(1,128)S(1)}, f32[1,2048,128]{2,1,0:T(8,128)S(1)}) %tuple.208, (bf16[2048,128]{1,0:T(8,128)(2,1)}, ...), branch_computations={%region_1.1_spmd, %region_2.6_spmd.clone, %region_7.0_spmd.clone} | conditional | flops 546057728 | bytes 19403572 | solution.py:94
  457.2 1.3 constant_dynamic-slice_fusion.2
  458.5 18.9 %while.104 = (s32[]{:T(128)}, f32[4,512]{1,0:T(4,128)S(1)}, f32[4,512]{1,0:T(4,128)S(1)}, f32[4,512,128]{2,1,0:T(8,128)S(1)}, s32[4]{0:T(128)S(1)}, /*index=5*/b...) while((s32[]{:T(128)}, f32[4,512]{1,0:T(4,128)S(1)}, ...), condition=%wide.region_11.10_spmd, body=%wide.region_8.9_spmd.sunk | while | flops 545259008 | bytes 14045825 | solution.py:38
  459.8 1.9 fusion.60
  464.5 1.9 fusion.60
  469.2 1.9 fusion.60
  474.0 1.9 fusion.60
  477.5 0.9 fusion.34
  509.5 1.1 fusion.35
  (103 shorter events, 23.4 us)
Async XLA Ops:
  6.5 0.8 copy-start
  6.5 101.5 %copy-start.1 = (s32[16,3]{0,1:T(4,128)S(1)}, s32[16,3]{0,1:T(4,128)}, u32[]{:S(2)}) copy-start(s32[16,3]{0,1:T(4,128)} %param.22) | copy-start | bytes 580
  6.5 233.9 %all-gather.3.cloned.1.call-start = ((), (), s32[]{:S(2)}) async-start(), calls=%async_computation.2 | async-start | bytes 8912896 | tf_op jit(solution)/shard_map/all_gather | solution.py:121
  52.0 362.3 %all-gather.5.cloned.1.call-start = ((), (), s32[]{:S(2)}) async-start(), calls=%async_computation.3 | async-start | bytes 8912896 | tf_op jit(solution)/shard_map/all_gather | solution.py:122
Sparse Core Ops, SparseCore 0:
  52.1 188.2 all-gather.2
  243.8 170.4 all-gather.4
where the time goes:
time: 518 us; the launch traced here: 517 us
  waiting for transfers between devices  306 us (59%)
  blocking collectives  99.4 us (19%)
  loops' own time  31.6 us (6%)
  matrix products  31 us (6%)
  local copies, waits for them, and re-layouts  20.1 us (4%)
  other arithmetic  15.7 us (3%)
  between operations  13.5 us (3%)
    all_gather x1, waiting for transfers between devices, on_device(): lax.all_gather(value_local, 'ctx', axis=0, tiled=True)  174 us
    all_gather x1, waiting for transfers between devices, on_device(): lax.all_gather(key_local, 'ctx', axis=0, tiled=True)  132 us
    all_to_all x1, blocking collectives, on_device(): lax.all_to_all(spread_values, 'head', split_axis=1, concat_axis=0, tiled=...  55 us
    all_to_all x1, blocking collectives, on_device(): lax.all_to_all(spread_keys, 'head', split_axis=1, concat_axis=0, tiled=True)  44.5 us
    another operation x1, loops' own time, fold_step(): return lax.fori_loop(0, key_piece.shape[0] // BLOCK, over, state)  30.8 us
    dot_general x12, matrix products, one_tile(): lax.dot_general(rows_q, key_block, (((1,), (1,)), ((), ())), preferred_el...  21 us
    slice x16, local copies, waits for them, and re-layouts, over(): listed[2] == block_pos  10.4 us
  transfers between devices with their start and end apart: 2, of which 2 were waited for; matrix products, arithmetic and copies ran while one was open for 0% of the time, Pallas kernels for 0%

commit v1 on v0

v1 whole, which is shorter than its diff:
```python
import functools

import jax
import jax.numpy as jnp
from jax import lax
from jax.experimental import pallas as pl
from jax.experimental.pallas import tpu as pltpu
from jax.sharding import PartitionSpec as P

DH = 128
BLOCK = 2048
SLOTS = 3
MESH = pl.DeviceIdType.MESH
LOG2E = 1.4426950408889634


def place():
    ctx = lax.axis_index("ctx")
    head = lax.axis_index("head")
    half, pair = ctx // 8, ctx % 8
    y, zlow = head // 8, head % 8
    return half, pair // 2, pair % 2, y, zlow


def device(half, pair, y, zlow):
    return (half * 8 + pair, y * 8 + zlow)


def spread_kernel(sel_ref, k_ref, v_ref, out_ref, ring, picked, landed,
                  a_send, a_recv, up_send, up_recv, down_send, down_recv, c_send, c_recv, o_sem):
    half, x, core, y, zlow = place()
    pair = x * 2 + core
    z = half * 8 + zlow
    above, below = (z + 1) % 16, (z + 15) % 16

    barrier = pltpu.get_barrier_semaphore()

    def hello(target):
        pl.semaphore_signal(barrier, inc=1, device_id=target, device_id_type=MESH)

    for src in range(8):
        @pl.when(jnp.logical_or(src != pair, x != y))
        def _():
            hello(device(half, src, x, zlow))
    hello(device(above // 8, pair, y, above % 8))
    hello(device(below // 8, pair, y, below % 8))
    for i in range(1, 8):
        hello(device(half, (pair + i) % 8, y, zlow))
    pl.semaphore_wait(barrier, jnp.where(x == y, 16, 17))

    def a_copy(kv, head, src, rows):
        return pltpu.make_async_remote_copy(
            src_ref=rows.at[:, pl.ds(head * DH, DH)],
            dst_ref=ring.at[z, src],
            send_sem=a_send.at[kv, head],
            recv_sem=a_recv.at[src],
            device_id=device(half, y * 2 + kv, head, zlow),
            device_id_type=MESH,
        )

    for kv, rows in ((0, k_ref), (1, v_ref)):
        for head in range(4):
            mine = jnp.logical_and(x == y, jnp.logical_and(core == kv, head == y))

            @pl.when(mine)
            def _():
                pltpu.make_async_copy(
                    rows.at[:, pl.ds(head * DH, DH)], ring.at[z, pair], a_recv.at[pair]
                ).start()

            @pl.when(jnp.logical_not(mine))
            def _():
                a_copy(kv, head, pair, rows).start()
    for src in range(8):
        pltpu.make_async_copy(ring.at[z, src], ring.at[z, src], a_recv.at[src]).wait()
    for kv, rows in ((0, k_ref), (1, v_ref)):
        for head in range(4):
            mine = jnp.logical_and(x == y, jnp.logical_and(core == kv, head == y))

            @pl.when(jnp.logical_not(mine))
            def _():
                a_copy(kv, head, pair, rows).wait_send()

    def r_copy(step, part, up):
        piece = (z + 16 - step) % 16 if up else (z + step) % 16
        to = above if up else below
        rows = ring.at[piece, pl.ds(part * 4, 4)]
        return pltpu.make_async_remote_copy(
            src_ref=rows,
            dst_ref=rows,
            send_sem=(up_send if up else down_send).at[step, part],
            recv_sem=(up_recv if up else down_recv).at[step, part],
            device_id=device(to // 8, pair, y, to % 8),
            device_id_type=MESH,
        )

    def r_wait(step, part, up):
        piece = (z + 16 - step - 1) % 16 if up else (z + step + 1) % 16
        rows = ring.at[piece, pl.ds(part * 4, 4)]
        pltpu.make_async_copy(rows, rows, (up_recv if up else down_recv).at[step, part]).wait()

    for step in range(8):
        for part in range(2):
            for up in (True, False):
                if not up and step == 7:
                    continue
                if step:
                    r_wait(step - 1, part, up)
                r_copy(step, part, up).start()
    for part in range(2):
        r_wait(7, part, True)
        r_wait(6, part, False)
    for step in range(8):
        for part in range(2):
            for up in (True, False):
                if not up and step == 7:
                    continue
                r_copy(step, part, up).wait_send()

    def c_copy(i, target, source):
        return pltpu.make_async_remote_copy(
            src_ref=picked.at[i - 1],
            dst_ref=landed.at[core, :, pl.ds(pl.multiple_of(x * 512, 512), 512)],
            send_sem=c_send.at[i - 1],
            recv_sem=c_recv.at[i - 1],
            device_id=device(half, target, y, zlow),
            device_id_type=MESH,
        )

    for i in (4, 3, 5, 2, 6, 1, 7, 0):
        target = (pair + i) % 8
        for slot in range(SLOTS):
            block = jnp.maximum(sel_ref[half * 8 + target, slot], 0)
            for piece in range(8):
                rows = ring[(block // 8) * 8 + piece, block % 8]
                if i:
                    picked[i - 1, slot, piece * 64:(piece + 1) * 64] = rows
                else:
                    landed[core, slot, pl.ds(pl.multiple_of(x * 512 + piece * 64, 64), 64)] = rows
        if i:
            c_copy(i, target, pair).start()
    for i in (4, 3, 5, 2, 6, 1, 7):
        source = (pair + 8 - i) % 8
        rows = landed.at[source % 2, :, pl.ds(pl.multiple_of(source // 2 * 512, 512), 512)]
        pltpu.make_async_copy(rows, rows, c_recv.at[i - 1]).wait()
        c_copy(i, (pair + i) % 8, pair).wait_send()
    copy = pltpu.make_async_copy(landed, out_ref, o_sem)
    copy.start()
    copy.wait()


def spread(key_rows, value_rows, selection):
    dma = pltpu.SemaphoreType.DMA
    return pl.pallas_call(
        spread_kernel,
        out_shape=jax.ShapeDtypeStruct((2, SLOTS, BLOCK, DH), jnp.bfloat16),
        in_specs=[
            pl.BlockSpec(memory_space=pltpu.SMEM),
            pl.BlockSpec(memory_space=pltpu.VMEM),
            pl.BlockSpec(memory_space=pltpu.VMEM),
        ],
        out_specs=pl.BlockSpec(memory_space=pl.ANY),
        scratch_shapes=[
            pltpu.VMEM((16, 8, 64, DH), jnp.bfloat16),
            pltpu.VMEM((7, SLOTS, 512, DH), jnp.bfloat16),
            pltpu.VMEM((2, SLOTS, BLOCK, DH), jnp.bfloat16),
            dma((2, 4)), dma((8,)),
            dma((8, 2)), dma((8, 2)), dma((8, 2)), dma((8, 2)),
            dma((7,)), dma((7,)), dma,
        ],
        compiler_params=pltpu.CompilerParams(
            collective_id=0, has_side_effects=True, vmem_limit_bytes=48 * 2**20
        ),
        name="spread_blocks",
    )(selection, key_rows, value_rows)


def attend_kernel(bq, bk, sel_ref, q_ref, kv_ref, out_ref, acc):
    ctx = lax.axis_index("ctx")
    tile = pl.program_id(0)
    factor = DH**-0.5 * LOG2E
    q = q_ref[...]

    acc[...] = jnp.zeros_like(acc)
    peak0 = jnp.full((bq, 128), -1e30, jnp.float32)

    def block_step(slot, chunk, peak, causal):
        start = pl.multiple_of(chunk * bk, bk)
        keys = kv_ref[0, slot, pl.ds(start, bk)]
        values = kv_ref[1, slot, pl.ds(start, bk)]
        scores = lax.dot_general(
            q, keys, (((1,), (1,)), ((), ())), preferred_element_type=jnp.float32
        )
        if causal:
            rows = lax.broadcasted_iota(jnp.int32, scores.shape, 0) + tile * bq
            cols = lax.broadcasted_iota(jnp.int32, scores.shape, 1) + start
            scores = jnp.where(cols <= rows, scores, -1e30)
        top = jnp.maximum(peak, jnp.max(scores, axis=1, keepdims=True))
        weights = jnp.exp2(scores * factor - (top * factor)[:, :1]).astype(jnp.bfloat16)
        widened = jnp.concatenate([values, jnp.ones_like(values)], axis=1)
        before = jnp.exp2((peak - top) * factor)[:, :1]
        acc[...] = acc[...] * before + jnp.dot(
            weights, widened, preferred_element_type=jnp.float32
        )
        return top

    def full(i, peak):
        return block_step(0, i, peak, False)

    peak = lax.fori_loop(0, tile * bq // bk, full, peak0)
    peak = block_step(0, tile * bq // bk, peak, True)
    for slot in range(1, SLOTS):
        live = sel_ref[ctx, slot] >= 0

        def more(i, peak):
            return block_step(slot, i, peak, False)

        peak = lax.fori_loop(0, jnp.where(live, BLOCK // bk, 0), more, peak)
    out_ref[...] = (acc[:, :DH] / acc[:, DH:]).astype(out_ref.dtype)


def attend(query_rows, kv, selection, bq=512, bk=512):
    return pl.pallas_call(
        functools.partial(attend_kernel, bq, bk),
        out_shape=jax.ShapeDtypeStruct(query_rows.shape, jnp.bfloat16),
        grid=(BLOCK // bq,),
        in_specs=[
            pl.BlockSpec(memory_space=pltpu.SMEM),
            pl.BlockSpec((bq, DH), lambda i: (i, 0)),
            pl.BlockSpec((2, SLOTS, BLOCK, DH), lambda i: (0, 0, 0, 0)),
        ],
        out_specs=pl.BlockSpec((bq, DH), lambda i: (i, 0)),
        scratch_shapes=[pltpu.VMEM((bq, 2 * DH), jnp.float32)],
        compiler_params=pltpu.CompilerParams(vmem_limit_bytes=40 * 2**20),
        name="attend_blocks",
    )(selection, query_rows, kv)


def on_device(query_rows, key_rows, value_rows, selection):
    kv = spread(key_rows, value_rows, selection)
    return attend(query_rows, kv, selection)


def solution(mesh):
    placed = (P("ctx", "head"), P(("ctx", "head"), None), P(("ctx", "head"), None), P())
    return jax.shard_map(
        on_device, mesh=mesh, in_specs=placed, out_specs=P("ctx", "head"), check_vma=False
    )
```

time: 518 us -> 125 us (0.24)
  the two profiles are of different devices: /device:TPU:3 before, /device:TPU:26 now
where the time goes in v1:
time: 125 us; the launch traced here: 124 us
  Pallas kernels  122 us (98%)
  local copies, waits for them, and re-layouts  2.5 us (2%)
    pallas_call x1, Pallas kernels, spread(): pl.pallas_call(spread_kernel, out_shape=jax.ShapeDtypeStruct((2, SLOTS, B...  85.4 us
    pallas_call x1, Pallas kernels, attend(): pl.pallas_call(functools.partial(attend_kernel, bq, bk), out_shape=jax.Sh...  36.4 us

profile of v1, /device:TPU:26, one launch (start us, length us, event | category | flops | bytes accessed | tf_op | source)
XLA Modules:
  0.0 124.3 jit_solution(12063860029015941389)
XLA Ops:
  0.0 0.0 copy-start
  0.0 0.8 copy.6.sel_ref
  0.8 0.0 copy-start.1
  0.8 0.8 copy-done.1
  1.7 0.0 copy-start.2
  1.7 0.8 copy-done.2
  2.5 85.4 %spread_blocks.1.kv_ref = bf16[2,3,2048,128]{3,2,1,0:T(8,128)(2,1)S(1)} custom-call(s32[16,3]{1,0:T(8,128)S(1)} %copy.6.sel_ref, bf16[64,512]{1,0:T(8,128)(2,1)S(1)} %copy-done.1, bf16[64,512]{1,0:T(8,128)(2,1)S(1)} %copy-done.2), custom_call_target="tpu_custom_call" | custom-call | tf_op jit(solution)/shard_map/spread_blocks/pallas_call | solution.py:154
  87.9 0.0 copy-done
  87.9 36.4 %attend_blocks.1 = bf16[2048,128]{1,0:T(8,128)(2,1)} custom-call(s32[16,3]{1,0:T(8,128)S(1)} %copy.6.sel_ref, bf16[2048,128]{1,0:T(8,128)(2,1)S(1)} %copy-done, bf16[2,3,2048,128]{3,2,1,0:T(8,128)(2,1)S(1)} %spread_blocks.1.kv_ref), custom_call_target="tpu_custom_call" | custom-call | tf_op jit(solution)/shard_map/attend_blocks/pallas_call | solution.py:223
Async XLA Ops:
  0.0 87.9 %copy-start = (bf16[2048,128]{1,0:T(8,128)(2,1)S(1)}, bf16[2048,128]{1,0:T(8,128)(2,1)}, u32[]{:S(2)}) copy-start(bf16[2048,128]{1,0:T(8,128)(2,1)} %q_ref.1) | copy-start | bytes 1572868
  0.8 0.8 copy-start.1
  1.7 0.8 copy-start.2

commit v2 on v0

v2 whole, which is shorter than its diff:
```python
import functools

import jax
import jax.numpy as jnp
from jax import lax
from jax.experimental import pallas as pl
from jax.experimental.pallas import tpu as pltpu
from jax.sharding import PartitionSpec as P

DH = 128
BLOCK = 2048
SLOTS = 3
PARTS = 4
TILE = 256
MESH = pl.DeviceIdType.MESH
FACTOR = DH**-0.5 * 1.4426950408889634
ROUNDS = (
    ("U4", "D4"), ("D3", "U5"), ("U3", "D5"), ("D2", "U6"),
    ("U2", "D6"), ("D1", "U7"), ("U1", "D7"), ("U0", "U8"),
)


def place():
    ctx = lax.axis_index("ctx")
    head = lax.axis_index("head")
    half, pair = ctx // 8, ctx % 8
    y, zlow = head // 8, head % 8
    return half, pair // 2, pair % 2, y, zlow


def device(half, pair, y, zlow):
    return (half * 8 + pair, y * 8 + zlow)


def fused_kernel(sel_hbm, q_hbm, k_hbm, v_hbm, out_ref, *scratch):
    ups, downs = scratch[:9], scratch[9:16]
    (sel_ref, q_ref, picked, land0, land, nat, peak, acc, l_sem,
     a_send, a_recv, up_send, up_recv, down_send, down_recv,
     o_send, o_recv, c_send, c_recv) = scratch[16:]
    half, x, core, y, zlow = place()
    ctx = lax.axis_index("ctx")
    pair = x * 2 + core
    z = half * 8 + zlow
    above, below = (z + 1) % 16, (z + 15) % 16

    def buffer(name):
        return ups[int(name[1])] if name[0] == "U" else downs[int(name[1]) - 1]

    def half_of(name):
        s = int(name[1])
        return ((z + 16 - s) % 16 if name[0] == "U" else (z + s) % 16) // 8

    load_sel = pltpu.make_async_copy(sel_hbm, sel_ref, l_sem.at[0])
    load_sel.start()
    load_q = pltpu.make_async_copy(q_hbm, q_ref, l_sem.at[1])
    load_q.start()

    barrier = pltpu.get_barrier_semaphore()

    def hello(target):
        pl.semaphore_signal(barrier, inc=1, device_id=target, device_id_type=MESH)

    for src in range(8):
        for part in range(2):
            origin = (x + 8 - src // 2 - 2 * part) % 4

            @pl.when(jnp.logical_or(src != pair, origin != y))
            def _():
                hello(device(half, src, origin, zlow))
    hello(device(above // 8, pair, y, above % 8))
    hello(device(below // 8, pair, y, below % 8))
    for i in range(1, 8):
        hello(device(half, (pair + i) % 8, y, zlow))
    pl.semaphore_wait(barrier, jnp.where(y % 2 == 0, 24, 25))

    def a_copies():
        for kv, rows in ((0, k_hbm), (1, v_hbm)):
            for head in range(4):
                for part in range(2):
                    mine = jnp.logical_and(
                        (y + 2 * part) % 4 == 0, jnp.logical_and(core == kv, head == y)
                    )
                    src = rows.at[pl.ds(part * 32, 32), pl.ds(head * DH, DH)]
                    dst = ups[0].at[pair, pl.ds(part * 32, 32)]
                    yield mine, pltpu.make_async_copy(src, dst, a_recv.at[pair, part]), (
                        pltpu.make_async_remote_copy(
                            src_ref=src,
                            dst_ref=dst,
                            send_sem=a_send.at[kv, head, part],
                            recv_sem=a_recv.at[pair, part],
                            device_id=device(half, (x + y + 2 * part) % 4 * 2 + kv, head, zlow),
                            device_id_type=MESH,
                        )
                    )

    for mine, local, remote in a_copies():
        pl.when(mine)(local.start)
        pl.when(jnp.logical_not(mine))(remote.start)
    for src in range(8):
        for part in range(2):
            rows = ups[0].at[src, pl.ds(part * 32, 32)]
            pltpu.make_async_copy(rows, rows, a_recv.at[src, part]).wait()
    load_sel.wait()

    width = 8 // PARTS

    def ring_copy(step, part, up):
        bufs = ups if up else (ups[0],) + tuple(downs)
        to = above if up else below
        return pltpu.make_async_remote_copy(
            src_ref=bufs[step].at[pl.ds(part * width, width)],
            dst_ref=bufs[step + 1].at[pl.ds(part * width, width)],
            send_sem=(up_send if up else down_send).at[step, part],
            recv_sem=(up_recv if up else down_recv).at[step, part],
            device_id=device(to // 8, pair, y, to % 8),
            device_id_type=MESH,
        )

    def own_sends(name, zpos):
        buf = buffer(name)
        rows = pl.ds(pl.multiple_of(zpos * 64, 64), 64)
        for i in (4, 3, 5, 2, 6, 1, 7):
            target = (pair + i) % 8
            pltpu.make_async_remote_copy(
                src_ref=buf.at[target],
                dst_ref=land0.at[core, x, rows],
                send_sem=o_send.at[i - 1],
                recv_sem=o_recv.at[i - 1],
                device_id=device(half, target, y, zlow),
                device_id_type=MESH,
            ).start()
        land0[core, x, rows] = buf[pair]

    def picked_copy(i, t):
        return pltpu.make_async_remote_copy(
            src_ref=picked.at[i - 1, t],
            dst_ref=land.at[core, t, :, x],
            send_sem=c_send.at[i - 1, t],
            recv_sem=c_recv.at[i - 1, t],
            device_id=device(half, (pair + i) % 8, y, zlow),
            device_id_type=MESH,
        )

    def picked_sends(t):
        one, two = ROUNDS[t]
        for i in (4, 3, 5, 2, 6, 1, 7, 0):
            target = (pair + i) % 8
            for slot in range(2):
                block = jnp.maximum(sel_ref[slot + 1, half * 8 + target], 0)
                rows = jnp.where(
                    block // 8 == half_of(one), buffer(one)[block % 8], buffer(two)[block % 8]
                )
                if i:
                    picked[i - 1, t, slot] = rows
                else:
                    land[core, t, slot, x] = rows
            if i:
                picked_copy(i, t).start()

    for step in range(9):
        for part in range(PARTS):
            for up in (True, False):
                last = 8 if up else 7
                if 0 < step <= last:
                    ring_copy(step - 1, part, up).wait_recv()
                if step < last:
                    ring_copy(step, part, up).start()
        if step == 0:
            own_sends("U0", zlow)
        elif step < 8:
            pl.when(zlow >= step)(functools.partial(own_sends, "U%d" % step, zlow - step))
            pl.when(zlow + step < 8)(functools.partial(own_sends, "D%d" % step, zlow + step))
        for t in range(8):
            if step == 4 + (t + 1) // 2:
                picked_sends(t)

    load_q.wait()
    for i in range(1, 8):
        src = (pair + 8 - i) % 8
        rows = land0.at[src % 2, src // 2]
        pltpu.make_async_copy(rows, rows, o_recv.at[i - 1]).wait()
    for src in range(4):
        for part in range(2):
            origin = (src + 8 - x - 2 * part) % 4

            def settle(zpos, _):
                start = pl.multiple_of(zpos * 64 + part * 32, 32)
                there = pl.multiple_of(origin * 512 + zpos * 64 + part * 32, 32)
                for kv in range(2):
                    nat[kv, pl.ds(there, 32)] = land0[kv, src, pl.ds(start, 32)]
                return 0

            lax.fori_loop(0, 8, settle, 0)

    def scores_of(q, keys):
        return lax.dot_general(
            q, keys, (((1,), (1,)), ((), ())), preferred_element_type=jnp.float32
        )

    def widened(values):
        return jnp.concatenate([values, jnp.ones_like(values)], axis=1)

    if True:
        for tile in range(BLOCK // TILE):
            rows = pl.ds(tile * TILE, TILE)
            count = (tile + 1) * TILE
            scores = scores_of(q_ref[rows], nat[0, :count])
            row_ids = lax.broadcasted_iota(jnp.int32, (TILE, TILE), 0)
            col_ids = lax.broadcasted_iota(jnp.int32, (TILE, TILE), 1)
            edge = jnp.where(col_ids <= row_ids, scores[:, count - TILE:], -1e30)
            scores = jnp.concatenate([scores[:, :count - TILE], edge], axis=1) if tile else edge
            top = jnp.max(scores, axis=1, keepdims=True)
            weights = jnp.exp2((scores - top) * FACTOR).astype(jnp.bfloat16)
            peak[rows] = jnp.broadcast_to(top, (TILE, DH))
            acc[rows] = jnp.dot(weights, widened(nat[1, :count]), preferred_element_type=jnp.float32)

    def absorb(t, masked):
        keys = land[0, t].reshape(512, DH)
        values = widened(land[1, t].reshape(512, DH))
        for tile in range(BLOCK // TILE):
            rows = pl.ds(tile * TILE, TILE)
            scores = scores_of(q_ref[rows], keys)
            if masked:
                cols = lax.broadcasted_iota(jnp.int32, scores.shape, 1)
                chosen = jnp.where(cols < 256, sel_ref[1, ctx], sel_ref[2, ctx])
                scores = jnp.where(chosen >= 0, scores, -1e30)
            old = peak[rows]
            top = jnp.maximum(old, jnp.max(scores, axis=1, keepdims=True))
            weights = jnp.exp2((scores - top[:, :1]) * FACTOR).astype(jnp.bfloat16)
            before = jnp.exp2((old - top) * FACTOR)
            peak[rows] = top
            acc[rows] = acc[rows] * jnp.concatenate([before, before], axis=1) + jnp.dot(
                weights, values, preferred_element_type=jnp.float32
            )

    def round_of(t, _):
        for i in range(1, 8):
            src = (pair + 8 - i) % 8
            rows = land.at[src % 2, t, :, src // 2]
            pltpu.make_async_copy(rows, rows, c_recv.at[i - 1, t]).wait()
        pl.when(ctx < 2)(lambda: absorb(t, True))
        pl.when(ctx >= 2)(lambda: absorb(t, False))
        return 0

    lax.fori_loop(0, 8, round_of, 0)
    for tile in range(BLOCK // TILE):
        rows = pl.ds(tile * TILE, TILE)
        out_ref[rows] = (acc[rows, :DH] / acc[rows, DH:]).astype(out_ref.dtype)

    for mine, local, remote in a_copies():
        pl.when(jnp.logical_not(mine))(remote.wait_send)
    for step in range(8):
        for part in range(PARTS):
            ring_copy(step, part, True).wait_send()
            if step < 7:
                ring_copy(step, part, False).wait_send()
    for i in range(1, 8):
        pltpu.make_async_copy(land0.at[0, 0], land0.at[0, 0], o_send.at[i - 1]).wait()
        for t in range(8):
            picked_copy(i, t).wait_send()


def fused(query_rows, key_rows, value_rows, selection):
    dma = pltpu.SemaphoreType.DMA
    anywhere = pl.BlockSpec(memory_space=pl.ANY)
    bf16 = jnp.bfloat16
    return pl.pallas_call(
        fused_kernel,
        out_shape=jax.ShapeDtypeStruct((BLOCK, DH), bf16),
        in_specs=[anywhere] * 4,
        out_specs=pl.BlockSpec(memory_space=pltpu.VMEM),
        scratch_shapes=[pltpu.VMEM((8, 64, DH), bf16)] * 16 + [
            pltpu.SMEM((SLOTS, 16), jnp.int32),
            pltpu.VMEM((BLOCK, DH), bf16),
            pltpu.VMEM((7, 8, 2, 64, DH), bf16),
            pltpu.VMEM((2, 4, 512, DH), bf16),
            pltpu.VMEM((2, 8, 2, 4, 64, DH), bf16),
            pltpu.VMEM((2, BLOCK, DH), bf16),
            pltpu.VMEM((BLOCK, DH), jnp.float32),
            pltpu.VMEM((BLOCK, 2 * DH), jnp.float32),
            dma((2,)),
            dma((2, 4, 2)), dma((8, 2)),
            dma((8, PARTS)), dma((8, PARTS)), dma((8, PARTS)), dma((8, PARTS)),
            dma((7,)), dma((7,)), dma((7, 8)), dma((7, 8)),
        ],
        compiler_params=pltpu.CompilerParams(
            collective_id=0, has_side_effects=True, vmem_limit_bytes=60 * 2**20
        ),
        name="block_attention",
    )(selection.T, query_rows, key_rows, value_rows)


def solution(mesh):
    placed = (P("ctx", "head"), P(("ctx", "head"), None), P(("ctx", "head"), None), P())
    return jax.shard_map(
        fused, mesh=mesh, in_specs=placed, out_specs=P("ctx", "head"), check_vma=False
    )
```

time: 518 us -> 87.5 us (0.17)
  the two profiles are of different devices: /device:TPU:3 before, /device:TPU:1 now
where the time goes in v2:
time: 87.5 us; the launch traced here: 87.3 us
  Pallas kernels  85.4 us (98%)
  local copies, waits for them, and re-layouts  1.87 us (2%)
    pallas_call x1, Pallas kernels, fused(): pl.pallas_call(fused_kernel, out_shape=jax.ShapeDtypeStruct((BLOCK, DH),...  85.4 us
    unnamed x1, local copies, waits for them, and re-layouts  1.87 us

profile of v2, /device:TPU:1, one launch (start us, length us, event | category | flops | bytes accessed | tf_op | source)
XLA Modules:
  0.0 87.3 jit_solution(15951669051832109814)
XLA Ops:
  0.0 85.4 %block_attention.1 = bf16[2048,128]{1,0:T(8,128)(2,1)} custom-call(s32[3,16]{1,0:T(4,128)} %bitcast.1, bf16[2048,128]{1,0:T(8,128)(2,1)} %q_hbm.1, bf16[64,512]{1,0:T(8,128)(2,1)} %k_hbm.1, bf16[64,512]{1,0:T(8,128)(2,1)} %v_hbm.1), custom_call_target="tpu_custom_call" | custom-call | tf_op jit(solution)/shard_map/block_attention/pallas_call | solution.py:267
  85.4 1.9 %copy.6 = bf16[2048,128]{1,0:T(8,128)(2,1)} copy(bf16[2048,128]{1,0:T(8,128)(2,1)} %block_attention.1) | data formatting | bytes 1048576

commit v3 on v2

v3 whole, which is shorter than its diff:
```python
import jax
import jax.numpy as jnp
from jax import lax
from jax.experimental import pallas as pl
from jax.experimental.pallas import tpu as pltpu
from jax.sharding import PartitionSpec as P

DH = 128
BLOCK = 2048
SLOTS = 3
PARTS = 4
TILE = 256
MESH = pl.DeviceIdType.MESH
FACTOR = DH**-0.5 * 1.4426950408889634
ROUNDS = (
    ("U4", "D4"), ("D3", "U5"), ("U3", "D5"), ("D2", "U6"),
    ("U2", "D6"), ("D1", "U7"), ("U1", "D7"), ("U0", "U8"),
)


def place():
    ctx = lax.axis_index("ctx")
    head = lax.axis_index("head")
    half, pair = ctx // 8, ctx % 8
    y, zlow = head // 8, head % 8
    return half, pair // 2, pair % 2, y, zlow


def device(half, pair, y, zlow):
    return (half * 8 + pair, y * 8 + zlow)


def fused_kernel(sel_hbm, q_hbm, k_hbm, v_hbm, out_ref, *scratch):
    ups, downs = scratch[:9], scratch[9:16]
    (sel_ref, q_ref, picked, land0, land, nat, peak, acc, l_sem,
     a_send, a_recv, up_send, up_recv, down_send, down_recv,
     o_send, o_recv, c_send, c_recv) = scratch[16:]
    half, x, core, y, zlow = place()
    ctx = lax.axis_index("ctx")
    pair = x * 2 + core
    z = half * 8 + zlow
    above, below = (z + 1) % 16, (z + 15) % 16
    early, late = half == 0, half == 1

    def buffer(name):
        return ups[int(name[1])] if name[0] == "U" else downs[int(name[1]) - 1]

    def half_of(name):
        s = int(name[1])
        return ((z + 16 - s) % 16 if name[0] == "U" else (z + s) % 16) // 8

    def in_line(name):
        s = int(name[1])
        return zlow >= s if name[0] == "U" else zlow + s < 8

    load_sel = pltpu.make_async_copy(sel_hbm, sel_ref, l_sem.at[0])
    load_sel.start()

    barrier = pltpu.get_barrier_semaphore()

    def hello(target):
        pl.semaphore_signal(barrier, inc=1, device_id=target, device_id_type=MESH)

    for src in range(8):
        for part in range(2):
            origin = (x + 8 - src // 2 - 2 * part) % 4

            @pl.when(jnp.logical_or(src != pair, origin != y))
            def _():
                hello(device(half, src, origin, zlow))
    hello(device(above // 8, pair, y, above % 8))
    hello(device(below // 8, pair, y, below % 8))
    for i in range(1, 8):
        hello(device(half, (pair + i) % 8, y, zlow))
    pl.semaphore_wait(barrier, jnp.where(y % 2 == 0, 24, 25))

    def first(act):
        for head in range(4):
            for part in range(2):
                for kv, rows in ((0, k_hbm), (1, v_hbm)):
                    mine = jnp.logical_and(
                        (y + 2 * part) % 4 == 0, jnp.logical_and(core == kv, head == y)
                    )
                    src = rows.at[pl.ds(part * 32, 32), pl.ds(head * DH, DH)]
                    dst = ups[0].at[pair, pl.ds(part * 32, 32)]

                    @pl.when(jnp.logical_not(mine))
                    def _():
                        copy = pltpu.make_async_remote_copy(
                            src_ref=src,
                            dst_ref=dst,
                            send_sem=a_send.at[kv, head, part],
                            recv_sem=a_recv.at[pair, part],
                            device_id=device(half, (x + y + 2 * part) % 4 * 2 + kv, head, zlow),
                            device_id_type=MESH,
                        )
                        copy.start() if act else copy.wait_send()

                    if act:
                        @pl.when(mine)
                        def _():
                            pltpu.make_async_copy(src, dst, a_recv.at[pair, part]).start()

    first(True)
    load_q = pltpu.make_async_copy(q_hbm, q_ref, l_sem.at[1])
    load_q.start()

    width = 8 // PARTS

    def ring_copy(step, part, up):
        bufs = ups if up else (ups[0],) + tuple(downs)
        to = above if up else below
        return pltpu.make_async_remote_copy(
            src_ref=bufs[step].at[pl.ds(part * width, width)],
            dst_ref=bufs[step + 1].at[pl.ds(part * width, width)],
            send_sem=(up_send if up else down_send).at[step, part],
            recv_sem=(up_recv if up else down_recv).at[step, part],
            device_id=device(to // 8, pair, y, to % 8),
            device_id_type=MESH,
        )

    def held(step, up):
        return jnp.logical_or(late, in_line(("U" if up else "D") + str(step)))

    def passed_on(step, up):
        edge = zlow == (7 if up else 0)
        return jnp.logical_and(held(step, up), jnp.logical_not(jnp.logical_and(late, edge)))

    def own_sends(name):
        buf = buffer(name)
        s = int(name[1])
        zpos = zlow - s if name[0] == "U" else zlow + s
        rows = pl.ds(pl.multiple_of(zpos * 64, 64), 64)
        for i in (4, 3, 5, 2, 6, 1, 7):
            target = (pair + i) % 8
            pltpu.make_async_remote_copy(
                src_ref=buf.at[target],
                dst_ref=land0.at[core, x, rows],
                send_sem=o_send.at[i - 1],
                recv_sem=o_recv.at[i - 1],
                device_id=device(half, target, y, zlow),
                device_id_type=MESH,
            ).start()
        land0[core, x, rows] = buf[pair]

    def picked_copy(i, t):
        return pltpu.make_async_remote_copy(
            src_ref=picked.at[i, t],
            dst_ref=land.at[core, t, :, x],
            send_sem=c_send.at[i, t],
            recv_sem=c_recv.at[i, t],
            device_id=device(half, (pair + i) % 8, y, zlow),
            device_id_type=MESH,
        )

    def block_for(row, slot):
        block = sel_ref[slot + 1, row]
        return jnp.maximum(jnp.where(block < 0, sel_ref[2 - slot, row], block), 0)

    def picked_sends(t, one, two=None):
        def rows_for(row, slot):
            block = block_for(row, slot)
            rows = buffer(one)[block % 8]
            if two is not None:
                rows = jnp.where(block // 8 == half_of(one), rows, buffer(two)[block % 8])
            return rows

        def to(n, _):
            i = (3 + n) % 7 + 1
            for slot in range(2):
                picked[i, t, slot] = rows_for(half * 8 + (pair + i) % 8, slot)
            picked_copy(i, t).start()
            return 0

        lax.fori_loop(0, 7, to, 0)
        for slot in range(2):
            land[core, t, slot, x] = rows_for(ctx, slot)

    turn = {}
    for t, names in enumerate(ROUNDS):
        for name in names:
            turn[name] = t

    for step in range(9):
        for part in range(PARTS):
            if step == 0:
                for src in range(part * width, (part + 1) * width):
                    for cut in range(2):
                        rows = ups[0].at[src, pl.ds(cut * 32, 32)]
                        pltpu.make_async_copy(rows, rows, a_recv.at[src, cut]).wait()
            for up in (True, False):
                last = 8 if up else 7
                if 0 < step <= last:
                    pl.when(held(step, up))(lambda: ring_copy(step - 1, part, up).wait_recv())
                if step < last:
                    pl.when(passed_on(step, up))(lambda: ring_copy(step, part, up).start())
        names = lambda s: ["U0"] if s == 0 else ["U%d" % s, "D%d" % s]
        if step == 0:
            load_sel.wait()
        if step < 8:
            for name in names(step):
                pl.when(in_line(name))(lambda: own_sends(name))
        if step > 0:
            for name in names(step - 1):
                pl.when(jnp.logical_and(early, in_line(name)))(
                    lambda: picked_sends(turn[name], name)
                )
        for t in range(8):
            if step == 4 + (t + 1) // 2:
                pl.when(late)(lambda: picked_sends(t, *ROUNDS[t]))

    load_q.wait()

    def scores_of(q, keys):
        return lax.dot_general(
            q, keys, (((1,), (1,)), ((), ())), preferred_element_type=jnp.float32
        )

    peak[...] = jnp.full_like(peak, -1e30)
    acc[...] = jnp.zeros_like(acc)

    def absorb(rows, scores, values):
        old = peak[rows]
        top = jnp.maximum(old, jnp.max(scores, axis=1, keepdims=True))
        weights = jnp.exp2((scores - top[:, :1]) * FACTOR).astype(jnp.bfloat16)
        before = jnp.exp2((old - top) * FACTOR)
        peak[rows] = top
        acc[rows] = acc[rows] * jnp.concatenate([before, before], axis=1) + jnp.dot(
            weights, values, preferred_element_type=jnp.float32
        )

    def own_block():
        for i in range(1, 8):
            src = (pair + 8 - i) % 8
            rows = land0.at[src % 2, src // 2]
            pltpu.make_async_copy(rows, rows, o_recv.at[i - 1]).wait()
        for src in range(4):
            for part in range(2):
                origin = (src + 8 - x - 2 * part) % 4

                def settle(zpos, _):
                    start = pl.multiple_of(zpos * 64 + part * 32, 32)
                    there = pl.multiple_of(origin * 512 + zpos * 64 + part * 32, 32)
                    for kv in range(2):
                        nat[kv, pl.ds(there, 32)] = land0[kv, src, pl.ds(start, 32)]
                    return 0

                lax.fori_loop(0, 8, settle, 0)
        for tile in range(BLOCK // TILE):
            rows = pl.ds(tile * TILE, TILE)
            count = (tile + 1) * TILE
            scores = scores_of(q_ref[rows], nat[0, :count])
            row_ids = lax.broadcasted_iota(jnp.int32, (TILE, TILE), 0)
            col_ids = lax.broadcasted_iota(jnp.int32, (TILE, TILE), 1)
            edge = jnp.where(col_ids <= row_ids, scores[:, count - TILE:], -1e30)
            scores = jnp.concatenate([scores[:, :count - TILE], edge], axis=1) if tile else edge
            values = nat[1, :count]
            absorb(rows, scores, jnp.concatenate([values, jnp.ones_like(values)], axis=1))

    def round_at(k):
        step = jnp.where(k % 2 == 1, -((k + 1) // 2), k // 2)
        near = jnp.minimum(zlow, 7 - zlow)
        far = jnp.where(zlow < 4, k - zlow, 7 - k - zlow)
        away = (jnp.where(k <= 2 * near, step, far) + 8) % 8
        return jnp.where(late, k, jnp.where(away <= 4, jnp.maximum(7 - 2 * away, 0), 2 * away - 8))

    def group(g):
        turns = [round_at(2 * g), round_at(2 * g + 1)]
        for t in turns:
            for i in range(1, 8):
                src = (pair + 8 - i) % 8
                rows = land.at[src % 2, t, :, src // 2]
                pltpu.make_async_copy(rows, rows, c_recv.at[i, t]).wait()

        @pl.when(ctx > 0)
        def _():
            slots = lax.broadcasted_iota(jnp.int32, (2, 256, DH), 0).reshape(512, DH)
            live = jnp.where(slots == 0, sel_ref[1, ctx], sel_ref[2, ctx]) >= 0
            ones = jnp.where(live, 1.0, 0.0).astype(jnp.bfloat16)
            keys = jnp.concatenate([land[0, t].reshape(512, DH) for t in turns], axis=0)
            values = jnp.concatenate(
                [
                    jnp.concatenate([land[1, t].reshape(512, DH) * ones, ones], axis=1)
                    for t in turns
                ],
                axis=0,
            )
            for tile in range(BLOCK // TILE):
                rows = pl.ds(tile * TILE, TILE)
                absorb(rows, scores_of(q_ref[rows], keys), values)

    own_turn = jnp.where(late, jnp.maximum(zlow, 7 - zlow) - 4, 3)

    def work(g, _):
        pl.when(g == own_turn)(own_block)
        group(g)
        return 0

    lax.fori_loop(0, 4, work, 0)
    for tile in range(BLOCK // TILE):
        rows = pl.ds(tile * TILE, TILE)
        out_ref[rows] = (acc[rows, :DH] / acc[rows, DH:]).astype(out_ref.dtype)

    first(False)
    for step in range(8):
        for up in (True, False):
            if up or step < 7:
                @pl.when(passed_on(step, up))
                def _():
                    for part in range(PARTS):
                        ring_copy(step, part, up).wait_send()
    for i in range(1, 8):
        pltpu.make_async_copy(land0.at[0, 0], land0.at[0, 0], o_send.at[i - 1]).wait()
        for t in range(8):
            picked_copy(i, t).wait_send()


def fused(query_rows, key_rows, value_rows, selection):
    dma = pltpu.SemaphoreType.DMA
    anywhere = pl.BlockSpec(memory_space=pl.ANY)
    bf16 = jnp.bfloat16
    return pl.pallas_call(
        fused_kernel,
        out_shape=jax.ShapeDtypeStruct((BLOCK, DH), bf16),
        in_specs=[anywhere] * 4,
        out_specs=pl.BlockSpec(memory_space=pltpu.VMEM),
        scratch_shapes=[pltpu.VMEM((8, 64, DH), bf16)] * 16 + [
            pltpu.SMEM((SLOTS, 16), jnp.int32),
            pltpu.VMEM((BLOCK, DH), bf16),
            pltpu.VMEM((8, 8, 2, 64, DH), bf16),
            pltpu.VMEM((2, 4, 512, DH), bf16),
            pltpu.VMEM((2, 8, 2, 4, 64, DH), bf16),
            pltpu.VMEM((2, BLOCK, DH), bf16),
            pltpu.VMEM((BLOCK, DH), jnp.float32),
            pltpu.VMEM((BLOCK, 2 * DH), jnp.float32),
            dma((2,)),
            dma((2, 4, 2)), dma((8, 2)),
            dma((8, PARTS)), dma((8, PARTS)), dma((8, PARTS)), dma((8, PARTS)),
            dma((7,)), dma((7,)), dma((8, 8)), dma((8, 8)),
        ],
        compiler_params=pltpu.CompilerParams(
            collective_id=0, has_side_effects=True, vmem_limit_bytes=60 * 2**20
        ),
        name="block_attention",
    )(selection.T, query_rows, key_rows, value_rows)


def solution(mesh):
    placed = (P("ctx", "head"), P(("ctx", "head"), None), P(("ctx", "head"), None), P())
    return jax.shard_map(
        fused, mesh=mesh, in_specs=placed, out_specs=P("ctx", "head"), check_vma=False
    )
```

time: 87.5 us -> 69.9 us (0.80)
  the two profiles are of different devices: /device:TPU:1 before, /device:TPU:481 now
where the time goes in v3:
time: 69.9 us; the launch traced here: 69.7 us
  Pallas kernels  67.8 us (97%)
  local copies, waits for them, and re-layouts  1.87 us (3%)
    pallas_call x1, Pallas kernels, fused(): pl.pallas_call(fused_kernel, out_shape=jax.ShapeDtypeStruct((BLOCK, DH),...  67.8 us
    unnamed x1, local copies, waits for them, and re-layouts  1.87 us

profile of v3, /device:TPU:481, one launch (start us, length us, event | category | flops | bytes accessed | tf_op | source)
XLA Modules:
  0.0 69.7 jit_solution(15769776719959400498)
XLA Ops:
  0.0 67.8 %block_attention.1 = bf16[2048,128]{1,0:T(8,128)(2,1)} custom-call(s32[3,16]{1,0:T(4,128)} %bitcast.1, bf16[2048,128]{1,0:T(8,128)(2,1)} %q_hbm.1, bf16[64,512]{1,0:T(8,128)(2,1)} %k_hbm.1, bf16[64,512]{1,0:T(8,128)(2,1)} %v_hbm.1), custom_call_target="tpu_custom_call" | custom-call | tf_op jit(solution)/shard_map/block_attention/pallas_call | solution.py:322
  67.8 1.9 %copy.6 = bf16[2048,128]{1,0:T(8,128)(2,1)} copy(bf16[2048,128]{1,0:T(8,128)(2,1)} %block_attention.1) | data formatting | bytes 1048576

commit v4 on v3

--- a/solution.py
+++ b/solution.py
@@ -1,3 +1,5 @@
+import functools
+
 import jax
 import jax.numpy as jnp
 from jax import lax
@@ -12,10 +14,7 @@
 TILE = 256
 MESH = pl.DeviceIdType.MESH
 FACTOR = DH**-0.5 * 1.4426950408889634
-ROUNDS = (
-    ("U4", "D4"), ("D3", "U5"), ("U3", "D5"), ("D2", "U6"),
-    ("U2", "D6"), ("D1", "U7"), ("U1", "D7"), ("U0", "U8"),
-)
+LEAST, MOST = 2.0**-80, 2.0**100
 
 
 def place():
@@ -30,11 +29,11 @@
     return (half * 8 + pair, y * 8 + zlow)
 
 
-def fused_kernel(sel_hbm, q_hbm, k_hbm, v_hbm, out_ref, *scratch):
+def fused_kernel(sel_hbm, q_hbm, k_hbm, v_hbm, out_ref, bad_ref, own_hbm, kv_hbm, *scratch):
     ups, downs = scratch[:9], scratch[9:16]
-    (sel_ref, q_ref, picked, land0, land, nat, peak, acc, l_sem,
+    (sel_ref, q_ref, picked, land0, land, nat, acc, l_sem, w_sem,
      a_send, a_recv, up_send, up_recv, down_send, down_recv,
-     o_send, o_recv, c_send, c_recv) = scratch[16:]
+     o_send, o_recv, c_send, c_recv, ready) = scratch[16:]
     half, x, core, y, zlow = place()
     ctx = lax.axis_index("ctx")
     pair = x * 2 + core
@@ -45,10 +44,6 @@
     def buffer(name):
         return ups[int(name[1])] if name[0] == "U" else downs[int(name[1]) - 1]
 
-    def half_of(name):
-        s = int(name[1])
-        return ((z + 16 - s) % 16 if name[0] == "U" else (z + s) % 16) // 8
-
     def in_line(name):
         s = int(name[1])
         return zlow >= s if name[0] == "U" else zlow + s < 8
@@ -68,11 +63,15 @@
             @pl.when(jnp.logical_or(src != pair, origin != y))
             def _():
                 hello(device(half, src, origin, zlow))
-    hello(device(above // 8, pair, y, above % 8))
+    pl.when(z < 15)(lambda: hello(device(above // 8, pair, y, above % 8)))
     hello(device(below // 8, pair, y, below % 8))
     for i in range(1, 8):
         hello(device(half, (pair + i) % 8, y, zlow))
-    pl.semaphore_wait(barrier, jnp.where(y % 2 == 0, 24, 25))
+    pl.semaphore_wait(barrier, 25 - jnp.where(y % 2 == 0, 1, 0) - jnp.where(z == 0, 1, 0))
+
+    @pl.when(z == 15)
+    def _():
+        pl.semaphore_signal(ready, inc=1, device_id=device(0, pair, y, 0), device_id_type=MESH)
 
     def first(act):
         for head in range(4):
@@ -157,31 +156,43 @@
         block = sel_ref[slot + 1, row]
         return jnp.maximum(jnp.where(block < 0, sel_ref[2 - slot, row], block), 0)
 
-    def picked_sends(t, one, two=None):
-        def rows_for(row, slot):
-            block = block_for(row, slot)
-            rows = buffer(one)[block % 8]
-            if two is not None:
-                rows = jnp.where(block // 8 == half_of(one), rows, buffer(two)[block % 8])
-            return rows
-
+    def picks(name, t, merge):
         def to(n, _):
-            i = (3 + n) % 7 + 1
+            i = (n + 4) % 8
             for slot in range(2):
-                picked[i, t, slot] = rows_for(half * 8 + (pair + i) % 8, slot)
-            picked_copy(i, t).start()
+                block = block_for(half * 8 + (pair + i) % 8, slot)
+                rows = buffer(name)[block % 8]
+                if merge:
+                    rows = jnp.where(block < 8, rows, picked[i, t, slot])
+                picked[i, t, slot] = rows
+            if merge:
+                pl.when(i > 0)(lambda: picked_copy(i, t).start())
+            else:
+                pl.when(jnp.logical_and(early, i > 0))(lambda: picked_copy(i, t).start())
             return 0
 
-        lax.fori_loop(0, 7, to, 0)
-        for slot in range(2):
-            land[core, t, slot, x] = rows_for(ctx, slot)
-
-    turn = {}
-    for t, names in enumerate(ROUNDS):
-        for name in names:
-            turn[name] = t
-
-    for step in range(9):
+        lax.fori_loop(0, 8, to, 0)
+
+        def keep():
+            for slot in range(2):
+                land[core, t, slot, x] = picked[0, t, slot]
+
+        keep() if merge else pl.when(early)(keep)
+
+    def turn(name, near):
+        s, r = int(name[1]), zlow
+        if name == "U0":
+            return 0
+        if near:
+            return s + (jnp.minimum(s - 1, 7 - r) if name[0] == "U" else jnp.minimum(s, r))
+        if name[0] == "U":
+            return s - r - 1 + jnp.maximum(0, s - 8 + r)
+        return s - 8 + r + jnp.maximum(0, s - r)
+
+    def names(s):
+        return ["U0"] if s == 0 else (["U%d" % s, "D%d" % s] if s < 8 else ["U8"])
+
+    def transfers(step):
         for part in range(PARTS):
             if step == 0:
                 for src in range(part * width, (part + 1) * width):
@@ -193,43 +204,45 @@
                 if 0 < step <= last:
                     pl.when(held(step, up))(lambda: ring_copy(step - 1, part, up).wait_recv())
                 if step < last:
-                    pl.when(passed_on(step, up))(lambda: ring_copy(step, part, up).start())
-        names = lambda s: ["U0"] if s == 0 else ["U%d" % s, "D%d" % s]
+                    go = passed_on(step, up)
+                    if step == 0 and not up:
+                        go = jnp.logical_and(go, z > 0)
+                    pl.when(go)(lambda: ring_copy(step, part, up).start())
         if step == 0:
             load_sel.wait()
         if step < 8:
             for name in names(step):
                 pl.when(in_line(name))(lambda: own_sends(name))
+        if step == 0:
+            @pl.when(z == 0)
+            def _():
+                pl.semaphore_wait(ready, 1)
+                for part in range(PARTS):
+                    ring_copy(0, part, False).start()
         if step > 0:
             for name in names(step - 1):
-                pl.when(jnp.logical_and(early, in_line(name)))(
-                    lambda: picked_sends(turn[name], name)
+                pl.when(in_line(name))(lambda: picks(name, turn(name, True), False))
+            for name in names(step):
+                pl.when(jnp.logical_and(late, jnp.logical_not(in_line(name))))(
+                    lambda: picks(name, turn(name, False), True)
                 )
-        for t in range(8):
-            if step == 4 + (t + 1) // 2:
-                pl.when(late)(lambda: picked_sends(t, *ROUNDS[t]))
-
-    load_q.wait()
 
     def scores_of(q, keys):
         return lax.dot_general(
             q, keys, (((1,), (1,)), ((), ())), preferred_element_type=jnp.float32
         )
 
-    peak[...] = jnp.full_like(peak, -1e30)
-    acc[...] = jnp.zeros_like(acc)
-
     def absorb(rows, scores, values):
-        old = peak[rows]
-        top = jnp.maximum(old, jnp.max(scores, axis=1, keepdims=True))
-        weights = jnp.exp2((scores - top[:, :1]) * FACTOR).astype(jnp.bfloat16)
-        before = jnp.exp2((old - top) * FACTOR)
-        peak[rows] = top
-        acc[rows] = acc[rows] * jnp.concatenate([before, before], axis=1) + jnp.dot(
-            weights, values, preferred_element_type=jnp.float32
-        )
-
-    def own_block():
+        weights = jnp.exp2(scores * FACTOR).astype(jnp.bfloat16)
+        acc[rows] += jnp.dot(weights, values, preferred_element_type=jnp.float32)
+
+    def keep_own(kv):
+        return pltpu.make_async_copy(nat.at[kv], own_hbm.at[kv], w_sem.at[kv, 8])
+
+    def keep_round(kv, t):
+        return pltpu.make_async_copy(land.at[kv, t], kv_hbm.at[kv, t], w_sem.at[kv, t])
+
+    def settle_own():
         for i in range(1, 8):
             src = (pair + 8 - i) % 8
             rows = land0.at[src % 2, src // 2]
@@ -246,7 +259,11 @@
                     return 0
 
                 lax.fori_loop(0, 8, settle, 0)
-        for tile in range(BLOCK // TILE):
+        for kv in range(2):
+            keep_own(kv).start()
+
+    def own_block(tiles):
+        for tile in tiles:
             rows = pl.ds(tile * TILE, TILE)
             count = (tile + 1) * TILE
             scores = scores_of(q_ref[rows], nat[0, :count])
@@ -257,50 +274,83 @@
             values = nat[1, :count]
             absorb(rows, scores, jnp.concatenate([values, jnp.ones_like(values)], axis=1))
 
-    def round_at(k):
-        step = jnp.where(k % 2 == 1, -((k + 1) // 2), k // 2)
-        near = jnp.minimum(zlow, 7 - zlow)
-        far = jnp.where(zlow < 4, k - zlow, 7 - k - zlow)
-        away = (jnp.where(k <= 2 * near, step, far) + 8) % 8
-        return jnp.where(late, k, jnp.where(away <= 4, jnp.maximum(7 - 2 * away, 0), 2 * away - 8))
-
-    def group(g):
-        turns = [round_at(2 * g), round_at(2 * g + 1)]
-        for t in turns:
-            for i in range(1, 8):
-                src = (pair + 8 - i) % 8
-                rows = land.at[src % 2, t, :, src // 2]
-                pltpu.make_async_copy(rows, rows, c_recv.at[i, t]).wait()
+    def wait_round(t):
+        for i in range(1, 8):
+            src = (pair + 8 - i) % 8
+            rows = land.at[src % 2, t, :, src // 2]
+            pltpu.make_async_copy(rows, rows, c_recv.at[i, t]).wait()
+        for kv in range(2):
+            keep_round(kv, t).start()
+
+    def rounds(first_of, count, base, tiles):
 
         @pl.when(ctx > 0)
         def _():
-            slots = lax.broadcasted_iota(jnp.int32, (2, 256, DH), 0).reshape(512, DH)
+            size = 512 * count
+            slots = lax.broadcasted_iota(jnp.int32, (2 * count, 256, DH), 0).reshape(size, DH) % 2
             live = jnp.where(slots == 0, sel_ref[1, ctx], sel_ref[2, ctx]) >= 0
             ones = jnp.where(live, 1.0, 0.0).astype(jnp.bfloat16)
-            keys = jnp.concatenate([land[0, t].reshape(512, DH) for t in turns], axis=0)
-            values = jnp.concatenate(
-                [
-                    jnp.concatenate([land[1, t].reshape(512, DH) * ones, ones], axis=1)
-                    for t in turns
-                ],
-                axis=0,
-            )
-            for tile in range(BLOCK // TILE):
-                rows = pl.ds(tile * TILE, TILE)
+            keys = land[0, pl.ds(first_of, count)].reshape(size, DH)
+            values = land[1, pl.ds(first_of, count)].reshape(size, DH)
+            values = jnp.concatenate([values * ones, ones], axis=1)
+            for tile in range(tiles):
+                rows = pl.ds(pl.multiple_of((base + tile) * TILE, TILE), TILE)
                 absorb(rows, scores_of(q_ref[rows], keys), values)
 
-    own_turn = jnp.where(late, jnp.maximum(zlow, 7 - zlow) - 4, 3)
-
-    def work(g, _):
-        pl.when(g == own_turn)(own_block)
-        group(g)
+    own_turn = 2 * jnp.where(late, jnp.maximum(zlow, 7 - zlow) - 4, 3)
+
+    start = jnp.where(own_turn >= 4, 3, 4)
+
+    def unit(u):
+        @pl.when(u == own_turn)
+        def _():
+            settle_own()
+            own_block(range(6))
+
+        pl.when(u == own_turn + 1)(lambda: own_block(range(6, 8)))
+
+        @pl.when(jnp.logical_and(u < 8, jnp.logical_or(u < own_turn, u > own_turn + 1)))
+        def _():
+            v = jnp.where(u < own_turn, u, u - 2)
+
+            @pl.when(v % 2 == 0)
+            def _():
+                wait_round(v)
+                wait_round(v + 1)
+
+            rounds(v // 2 * 2, 2, v % 2 * 4, 4)
+
+        @pl.when(u >= 8)
+        def _():
+            wait_round(u - 2)
+            rounds(u - 2, 1, 0, 8)
+
+    def turns(n, _):
+        for step in range(9):
+            pl.when(n == step)(functools.partial(transfers, step))
+
+        @pl.when(n == 0)
+        def _():
+            load_q.wait()
+            acc[...] = jnp.zeros_like(acc)
+
+        pl.when(jnp.logical_and(n >= start, n < start + 10))(lambda: unit(n - start))
         return 0
 
-    lax.fori_loop(0, 4, work, 0)
+    lax.fori_loop(0, 14, turns, 0)
+    bad_ref[...] = jnp.zeros_like(bad_ref)
     for tile in range(BLOCK // TILE):
         rows = pl.ds(tile * TILE, TILE)
-        out_ref[rows] = (acc[rows, :DH] / acc[rows, DH:]).astype(out_ref.dtype)
-
+        mass = acc[rows, DH:]
+        out_ref[rows] = (acc[rows, :DH] / mass).astype(out_ref.dtype)
+        fine = jnp.logical_and(mass > LEAST, mass < MOST)
+        marks = jnp.where(fine, 0.0, 1.0).reshape(TILE // 8, 8, DH)
+        bad_ref[...] = jnp.maximum(bad_ref[...], jnp.max(marks, axis=0))
+
+    for kv in range(2):
+        keep_own(kv).wait()
+        for t in range(8):
+            keep_round(kv, t).wait()
     first(False)
     for step in range(8):
         for up in (True, False):
@@ -321,9 +371,19 @@
     bf16 = jnp.bfloat16
     return pl.pallas_call(
         fused_kernel,
-        out_shape=jax.ShapeDtypeStruct((BLOCK, DH), bf16),
+        out_shape=(
+            jax.ShapeDtypeStruct((BLOCK, DH), bf16),
+            jax.ShapeDtypeStruct((8, DH), jnp.float32),
+            jax.ShapeDtypeStruct((2, BLOCK, DH), bf16),
+            jax.ShapeDtypeStruct((2, 8, 2, 4, 64, DH), bf16),
+        ),
         in_specs=[anywhere] * 4,
-        out_specs=pl.BlockSpec(memory_space=pltpu.VMEM),
+        out_specs=(
+            pl.BlockSpec(memory_space=pltpu.VMEM),
+            pl.BlockSpec(memory_space=pltpu.VMEM),
+            anywhere,
+            anywhere,
+        ),
         scratch_shapes=[pltpu.VMEM((8, 64, DH), bf16)] * 16 + [
             pltpu.SMEM((SLOTS, 16), jnp.int32),
             pltpu.VMEM((BLOCK, DH), bf16),
@@ -331,12 +391,12 @@
             pltpu.VMEM((2, 4, 512, DH), bf16),
             pltpu.VMEM((2, 8, 2, 4, 64, DH), bf16),
             pltpu.VMEM((2, BLOCK, DH), bf16),
-            pltpu.VMEM((BLOCK, DH), jnp.float32),
             pltpu.VMEM((BLOCK, 2 * DH), jnp.float32),
-            dma((2,)),
+            dma((2,)), dma((2, 9)),
             dma((2, 4, 2)), dma((8, 2)),
             dma((8, PARTS)), dma((8, PARTS)), dma((8, PARTS)), dma((8, PARTS)),
             dma((7,)), dma((7,)), dma((8, 8)), dma((8, 8)),
+            pltpu.SemaphoreType.REGULAR,
         ],
         compiler_params=pltpu.CompilerParams(
             collective_id=0, has_side_effects=True, vmem_limit_bytes=60 * 2**20
@@ -345,8 +405,92 @@
     )(selection.T, query_rows, key_rows, value_rows)
 
 
+def finish_kernel(
+    fast_ref, bad_ref, sel_hbm, q_hbm, own_hbm, kv_hbm, out_ref, sel_ref, q_ref, own, kv, acc, sem
+):
+    ctx = lax.axis_index("ctx")
+    step = pl.program_id(0)
+    size = fast_ref.shape[0]
+    marked = jnp.max(bad_ref[...]) > 0.0
+
+    @pl.when(jnp.logical_not(marked))
+    def _():
+        out_ref[...] = fast_ref[...]
+
+    @pl.when(jnp.logical_and(marked, step == 0))
+    def _():
+        pairs = ((sel_hbm, sel_ref), (q_hbm, q_ref), (own_hbm, own), (kv_hbm, kv))
+        copies = [pltpu.make_async_copy(a, b, sem.at[i]) for i, (a, b) in enumerate(pairs)]
+        for copy in copies:
+            copy.start()
+        for copy in copies:
+            copy.wait()
+
+    @pl.when(marked)
+    def _():
+        q = q_ref[pl.ds(pl.multiple_of(step * size, size), size)]
+        acc[...] = jnp.zeros_like(acc)
+
+        def absorb(keys, values, allowed, peak):
+            scores = lax.dot_general(
+                q, keys, (((1,), (1,)), ((), ())), preferred_element_type=jnp.float32
+            )
+            scores = jnp.where(allowed, scores, -1e30)
+            top = jnp.maximum(peak, jnp.max(scores, axis=1, keepdims=True))
+            weights = jnp.where(allowed, jnp.exp2((scores - top[:, :1]) * FACTOR), 0.0)
+            before = jnp.exp2((peak - top) * FACTOR)[:, :1]
+            wide = jnp.concatenate([values, jnp.ones_like(values)], axis=1)
+            acc[...] = acc[...] * before + jnp.dot(
+                weights.astype(jnp.bfloat16), wide, preferred_element_type=jnp.float32
+            )
+            return top
+
+        row_ids = lax.broadcasted_iota(jnp.int32, (size, 512), 0) + step * size
+        col_ids = lax.broadcasted_iota(jnp.int32, (size, 512), 1)
+
+        def own_part(i, peak):
+            there = pl.ds(pl.multiple_of(i * 512, 512), 512)
+            return absorb(own[0, there], own[1, there], col_ids + i * 512 <= row_ids, peak)
+
+        def round_part(t, peak):
+            live = jnp.where(col_ids < 256, sel_ref[1, ctx], sel_ref[2, ctx]) >= 0
+            return absorb(kv[0, t].reshape(512, DH), kv[1, t].reshape(512, DH), live, peak)
+
+        peak = jnp.full((size, DH), -1e30, jnp.float32)
+        peak = lax.fori_loop(0, (step + 1) * size // 512, own_part, peak)
+        lax.fori_loop(0, 8, round_part, peak)
+        out_ref[...] = (acc[:, :DH] / acc[:, DH:]).astype(out_ref.dtype)
+
+
+def attention(query_rows, key_rows, value_rows, selection):
+    fast, bad, own, kv = fused(query_rows, key_rows, value_rows, selection)
+    anywhere = pl.BlockSpec(memory_space=pl.ANY)
+    size = 1024
+    return pl.pallas_call(
+        finish_kernel,
+        out_shape=jax.ShapeDtypeStruct(fast.shape, fast.dtype),
+        grid=(BLOCK // size,),
+        in_specs=[
+            pl.BlockSpec((size, DH), lambda i: (i, 0)),
+            pl.BlockSpec((8, DH), lambda i: (0, 0)),
+            anywhere, anywhere, anywhere, anywhere,
+        ],
+        out_specs=pl.BlockSpec((size, DH), lambda i: (i, 0)),
+        scratch_shapes=[
+            pltpu.SMEM((SLOTS, 16), jnp.int32),
+            pltpu.VMEM((BLOCK, DH), jnp.bfloat16),
+            pltpu.VMEM((2, BLOCK, DH), jnp.bfloat16),
+            pltpu.VMEM((2, 8, 2, 4, 64, DH), jnp.bfloat16),
+            pltpu.VMEM((size, 2 * DH), jnp.float32),
+            pltpu.SemaphoreType.DMA((4,)),
+        ],
+        compiler_params=pltpu.CompilerParams(vmem_limit_bytes=60 * 2**20),
+        name="finish",
+    )(fast, bad, selection.T, query_rows, own, kv)
+
+
 def solution(mesh):
     placed = (P("ctx", "head"), P(("ctx", "head"), None), P(("ctx", "head"), None), P())
     return jax.shard_map(
-        fused, mesh=mesh, in_specs=placed, out_specs=P("ctx", "head"), check_vma=False
+        attention, mesh=mesh, in_specs=placed, out_specs=P("ctx", "head"), check_vma=False
     )

time: 69.9 us -> 97.7 us (1.40)
  the two profiles are of different devices: /device:TPU:481 before, /device:TPU:1 now
where the time goes in v4:
time: 97.7 us; the launch traced here: 96 us
  Pallas kernels  95.8 us (98%)
    pallas_call x1, Pallas kernels, fused(): pl.pallas_call(fused_kernel, out_shape=(jax.ShapeDtypeStruct((BLOCK, DH),...  62.6 us
    pallas_call x1, Pallas kernels, attention(): pl.pallas_call(finish_kernel, out_shape=jax.ShapeDtypeStruct(fast.shape,...  33.2 us

profile of v4, /device:TPU:1, one launch (start us, length us, event | category | flops | bytes accessed | tf_op | source)
XLA Modules:
  0.0 96.0 jit_solution(15425033268176279217)
XLA Ops:
  0.0 62.6 %block_attention.1 = (bf16[2048,128]{1,0:T(8,128)(2,1)}, f32[8,128]{1,0:T(8,128)}, bf16[2,2048,128]{2,1,0:T(8,128)(2,1)}, bf16[2,8,2,4,64,128]{5,4,3,2,1,0:T(8,128)(2,1)}) custom-call(s32[3,16]{1,0:T(4,128)} %bitcast.1, bf16[2048,128]{1,0:T(8,128)(2,1)} %q_hbm.3, bf16[64,512]{1,0:T(8,128)(2,1)} %k_hbm.1, bf16[64,512]{1,0:T(8,128)(2,1)} %v_hbm.1), custom_call_target="tpu_custom_call" | custom-call | tf_op jit(solution)/shard_map/block_attention/pallas_call | solution.py:372
  62.6 33.2 %finish.1 = bf16[2048,128]{1,0:T(8,128)(2,1)} custom-call(bf16[2048,128]{1,0:T(8,128)(2,1)} %get-tuple-element.9.fast_ref, f32[8,128]{1,0:T(8,128)} %get-tuple-element.10.bad_ref, s32[3,16]{1,0:T(4,128)} %bitcast.2, bf16[2048,128]{1,0:T(8,128)(2,1)} %q_hbm.3, bf16[2,2048,128]{2,1,0:T(8,128)(2,1)} %get-tuple-element.11.own_hbm, ...), custom_call_target="tpu_custom_call" | custom-call | tf_op jit(solution)/shard_map/finish/pallas_call | solution.py:469

commit v5 on v4

--- a/solution.py
+++ b/solution.py
@@ -14,6 +14,7 @@
 TILE = 256
 MESH = pl.DeviceIdType.MESH
 FACTOR = DH**-0.5 * 1.4426950408889634
+START = 6
 LEAST, MOST = 2.0**-80, 2.0**100
 
 
@@ -112,7 +113,7 @@
         return pltpu.make_async_remote_copy(
             src_ref=bufs[step].at[pl.ds(part * width, width)],
             dst_ref=bufs[step + 1].at[pl.ds(part * width, width)],
-            send_sem=(up_send if up else down_send).at[step, part],
+            send_sem=(up_send if up else down_send).at[step],
             recv_sem=(up_recv if up else down_recv).at[step, part],
             device_id=device(to // 8, pair, y, to % 8),
             device_id_type=MESH,
@@ -146,7 +147,7 @@
         return pltpu.make_async_remote_copy(
             src_ref=picked.at[i, t],
             dst_ref=land.at[core, t, :, x],
-            send_sem=c_send.at[i, t],
+            send_sem=c_send.at[i],
             recv_sem=c_recv.at[i, t],
             device_id=device(half, (pair + i) % 8, y, zlow),
             device_id_type=MESH,
@@ -219,9 +220,9 @@
                 pl.semaphore_wait(ready, 1)
                 for part in range(PARTS):
                     ring_copy(0, part, False).start()
+        for name in (names(step) if step < 4 else []) + (names(step - 1) if step > 4 else []):
+            pl.when(in_line(name))(lambda: picks(name, turn(name, True), False))
         if step > 0:
-            for name in names(step - 1):
-                pl.when(in_line(name))(lambda: picks(name, turn(name, True), False))
             for name in names(step):
                 pl.when(jnp.logical_and(late, jnp.logical_not(in_line(name))))(
                     lambda: picks(name, turn(name, False), True)
@@ -299,7 +300,6 @@
 
     own_turn = 2 * jnp.where(late, jnp.maximum(zlow, 7 - zlow) - 4, 3)
 
-    start = jnp.where(own_turn >= 4, 3, 4)
 
     def unit(u):
         @pl.when(u == own_turn)
@@ -325,6 +325,19 @@
             wait_round(u - 2)
             rounds(u - 2, 1, 0, 8)
 
+    def sent():
+        first(False)
+        for step in range(8):
+            for up in (True, False):
+                if up or step < 7:
+                    piece = (ups if up else (ups[0],) + tuple(downs))[step]
+                    semaphore = (up_send if up else down_send).at[step]
+                    pl.when(passed_on(step, up))(
+                        lambda: pltpu.make_async_copy(piece, piece, semaphore).wait()
+                    )
+        for i in range(1, 8):
+            pltpu.make_async_copy(land0.at[0, 0], land0.at[0, 0], o_send.at[i - 1]).wait()
+
     def turns(n, _):
         for step in range(9):
             pl.when(n == step)(functools.partial(transfers, step))
@@ -334,10 +347,11 @@
             load_q.wait()
             acc[...] = jnp.zeros_like(acc)
 
-        pl.when(jnp.logical_and(n >= start, n < start + 10))(lambda: unit(n - start))
+        pl.when(n == START + 7)(sent)
+        pl.when(n >= START)(lambda: unit(n - START))
         return 0
 
-    lax.fori_loop(0, 14, turns, 0)
+    lax.fori_loop(0, START + 10, turns, 0)
     bad_ref[...] = jnp.zeros_like(bad_ref)
     for tile in range(BLOCK // TILE):
         rows = pl.ds(tile * TILE, TILE)
@@ -351,18 +365,8 @@
         keep_own(kv).wait()
         for t in range(8):
             keep_round(kv, t).wait()
-    first(False)
-    for step in range(8):
-        for up in (True, False):
-            if up or step < 7:
-                @pl.when(passed_on(step, up))
-                def _():
-                    for part in range(PARTS):
-                        ring_copy(step, part, up).wait_send()
     for i in range(1, 8):
-        pltpu.make_async_copy(land0.at[0, 0], land0.at[0, 0], o_send.at[i - 1]).wait()
-        for t in range(8):
-            picked_copy(i, t).wait_send()
+        pltpu.make_async_copy(picked.at[i], picked.at[i], c_send.at[i]).wait()
 
 
 def fused(query_rows, key_rows, value_rows, selection):
@@ -394,8 +398,8 @@
             pltpu.VMEM((BLOCK, 2 * DH), jnp.float32),
             dma((2,)), dma((2, 9)),
             dma((2, 4, 2)), dma((8, 2)),
-            dma((8, PARTS)), dma((8, PARTS)), dma((8, PARTS)), dma((8, PARTS)),
-            dma((7,)), dma((7,)), dma((8, 8)), dma((8, 8)),
+            dma((8,)), dma((8, PARTS)), dma((8,)), dma((8, PARTS)),
+            dma((7,)), dma((7,)), dma((8,)), dma((8, 8)),
             pltpu.SemaphoreType.REGULAR,
         ],
         compiler_params=pltpu.CompilerParams(

time: 97.7 us -> 93.9 us (0.961); the launches traced: 96 us -> 93.7 us
  Pallas kernels: 95.8 us -> 93.5 us
    pallas_call x1, Pallas kernels: 62.6 us -> 60.3 us  [fused(): pl.pallas_call(fused_kernel, out_shape=(jax.ShapeDtypeStruct((BLOCK, DH),...]
where the time goes in v5:
time: 93.9 us; the launch traced here: 93.7 us
  Pallas kernels  93.5 us (100%)
    pallas_call x1, Pallas kernels, fused(): pl.pallas_call(fused_kernel, out_shape=(jax.ShapeDtypeStruct((BLOCK, DH),...  60.3 us
    pallas_call x1, Pallas kernels, attention(): pl.pallas_call(finish_kernel, out_shape=jax.ShapeDtypeStruct(fast.shape,...  33.2 us

profile of v5, /device:TPU:1, one launch (start us, length us, event | category | flops | bytes accessed | tf_op | source)
XLA Modules:
  0.0 93.7 jit_solution(9242241399711131853)
XLA Ops:
  0.0 60.3 %block_attention.1 = (bf16[2048,128]{1,0:T(8,128)(2,1)}, f32[8,128]{1,0:T(8,128)}, bf16[2,2048,128]{2,1,0:T(8,128)(2,1)}, bf16[2,8,2,4,64,128]{5,4,3,2,1,0:T(8,128)(2,1)}) custom-call(s32[3,16]{1,0:T(4,128)} %bitcast.1, bf16[2048,128]{1,0:T(8,128)(2,1)} %q_hbm.3, bf16[64,512]{1,0:T(8,128)(2,1)} %k_hbm.1, bf16[64,512]{1,0:T(8,128)(2,1)} %v_hbm.1), custom_call_target="tpu_custom_call" | custom-call | tf_op jit(solution)/shard_map/block_attention/pallas_call | solution.py:376
  60.4 33.2 %finish.1 = bf16[2048,128]{1,0:T(8,128)(2,1)} custom-call(bf16[2048,128]{1,0:T(8,128)(2,1)} %get-tuple-element.9.fast_ref, f32[8,128]{1,0:T(8,128)} %get-tuple-element.10.bad_ref, s32[3,16]{1,0:T(4,128)} %bitcast.2, bf16[2048,128]{1,0:T(8,128)(2,1)} %q_hbm.3, bf16[2,2048,128]{2,1,0:T(8,128)(2,1)} %get-tuple-element.11.own_hbm, ...), custom_call_target="tpu_custom_call" | custom-call | tf_op jit(solution)/shard_map/finish/pallas_call | solution.py:473

commit v6 on v5

--- a/solution.py
+++ b/solution.py
@@ -30,9 +30,9 @@
     return (half * 8 + pair, y * 8 + zlow)
 
 
-def fused_kernel(sel_hbm, q_hbm, k_hbm, v_hbm, out_ref, bad_ref, own_hbm, kv_hbm, *scratch):
+def fused_kernel(sel_hbm, q_hbm, k_hbm, v_hbm, out_hbm, bad_ref, own_hbm, kv_hbm, *scratch):
     ups, downs = scratch[:9], scratch[9:16]
-    (sel_ref, q_ref, picked, land0, land, nat, acc, l_sem, w_sem,
+    (sel_ref, q_ref, k_ref, v_ref, out_ref, picked, land0, land, nat, acc, l_sem, w_sem, e_sem,
      a_send, a_recv, up_send, up_recv, down_send, down_recv,
      o_send, o_recv, c_send, c_recv, ready) = scratch[16:]
     half, x, core, y, zlow = place()
@@ -51,6 +51,12 @@
 
     load_sel = pltpu.make_async_copy(sel_hbm, sel_ref, l_sem.at[0])
     load_sel.start()
+    load_rows = [
+        pltpu.make_async_copy(k_hbm, k_ref, l_sem.at[2]),
+        pltpu.make_async_copy(v_hbm, v_ref, l_sem.at[3]),
+    ]
+    for load in load_rows:
+        load.start()
 
     barrier = pltpu.get_barrier_semaphore()
 
@@ -77,7 +83,7 @@
     def first(act):
         for head in range(4):
             for part in range(2):
-                for kv, rows in ((0, k_hbm), (1, v_hbm)):
+                for kv, rows in ((0, k_ref), (1, v_ref)):
                     mine = jnp.logical_and(
                         (y + 2 * part) % 4 == 0, jnp.logical_and(core == kv, head == y)
                     )
@@ -101,6 +107,8 @@
                         def _():
                             pltpu.make_async_copy(src, dst, a_recv.at[pair, part]).start()
 
+    for load in load_rows:
+        load.wait()
     first(True)
     load_q = pltpu.make_async_copy(q_hbm, q_ref, l_sem.at[1])
     load_q.start()
@@ -146,7 +154,7 @@
     def picked_copy(i, t):
         return pltpu.make_async_remote_copy(
             src_ref=picked.at[i, t],
-            dst_ref=land.at[core, t, :, x],
+            dst_ref=land.at[core, t, x],
             send_sem=c_send.at[i],
             recv_sem=c_recv.at[i, t],
             device_id=device(half, (pair + i) % 8, y, zlow),
@@ -176,7 +184,7 @@
 
         def keep():
             for slot in range(2):
-                land[core, t, slot, x] = picked[0, t, slot]
+                land[core, t, x, slot] = picked[0, t, slot]
 
         keep() if merge else pl.when(early)(keep)
 
@@ -278,22 +286,24 @@
     def wait_round(t):
         for i in range(1, 8):
             src = (pair + 8 - i) % 8
-            rows = land.at[src % 2, t, :, src // 2]
+            rows = land.at[src % 2, t, src // 2]
             pltpu.make_async_copy(rows, rows, c_recv.at[i, t]).wait()
         for kv in range(2):
             keep_round(kv, t).start()
 
+    def operands(first_of, count):
+        size = 512 * count
+        slots = lax.broadcasted_iota(jnp.int32, (4 * count, 2, 64, DH), 1).reshape(size, DH)
+        live = jnp.where(slots == 0, sel_ref[1, ctx], sel_ref[2, ctx]) >= 0
+        ones = jnp.where(live, 1.0, 0.0).astype(jnp.bfloat16)
+        keys = land[0, pl.ds(first_of, count)].reshape(size, DH)
+        values = land[1, pl.ds(first_of, count)].reshape(size, DH)
+        return keys, jnp.concatenate([values * ones, ones], axis=1)
+
     def rounds(first_of, count, base, tiles):
-
         @pl.when(ctx > 0)
         def _():
-            size = 512 * count
-            slots = lax.broadcasted_iota(jnp.int32, (2 * count, 256, DH), 0).reshape(size, DH) % 2
-            live = jnp.where(slots == 0, sel_ref[1, ctx], sel_ref[2, ctx]) >= 0
-            ones = jnp.where(live, 1.0, 0.0).astype(jnp.bfloat16)
-            keys = land[0, pl.ds(first_of, count)].reshape(size, DH)
-            values = land[1, pl.ds(first_of, count)].reshape(size, DH)
-            values = jnp.concatenate([values * ones, ones], axis=1)
+            keys, values = operands(first_of, count)
             for tile in range(tiles):
                 rows = pl.ds(pl.multiple_of((base + tile) * TILE, TILE), TILE)
                 absorb(rows, scores_of(q_ref[rows], keys), values)
@@ -320,10 +330,10 @@
 
             rounds(v // 2 * 2, 2, v % 2 * 4, 4)
 
-        @pl.when(u >= 8)
+        @pl.when(u == 8)
         def _():
-            wait_round(u - 2)
-            rounds(u - 2, 1, 0, 8)
+            wait_round(6)
+            rounds(6, 1, 0, 8)
 
     def sent():
         first(False)
@@ -348,18 +358,30 @@
             acc[...] = jnp.zeros_like(acc)
 
         pl.when(n == START + 7)(sent)
-        pl.when(n >= START)(lambda: unit(n - START))
+        begun = n - START + jnp.where(z == 0, 1, 0)
+        pl.when(jnp.logical_and(begun >= 0, begun < 9))(lambda: unit(begun))
         return 0
 
-    lax.fori_loop(0, START + 10, turns, 0)
+    lax.fori_loop(0, START + 9, turns, 0)
     bad_ref[...] = jnp.zeros_like(bad_ref)
+    wait_round(7)
+    keys, values = operands(7, 1)
+    results = []
     for tile in range(BLOCK // TILE):
         rows = pl.ds(tile * TILE, TILE)
-        mass = acc[rows, DH:]
-        out_ref[rows] = (acc[rows, :DH] / mass).astype(out_ref.dtype)
+        weights = jnp.exp2(scores_of(q_ref[rows], keys) * FACTOR).astype(jnp.bfloat16)
+        total = acc[rows] + jnp.dot(weights, values, preferred_element_type=jnp.float32)
+        mass = total[:, DH:]
+        out_ref[rows] = (total[:, :DH] / mass).astype(out_ref.dtype)
         fine = jnp.logical_and(mass > LEAST, mass < MOST)
         marks = jnp.where(fine, 0.0, 1.0).reshape(TILE // 8, 8, DH)
         bad_ref[...] = jnp.maximum(bad_ref[...], jnp.max(marks, axis=0))
+        if tile % 2:
+            done = pl.ds((tile - 1) * TILE, 2 * TILE)
+            results.append(
+                pltpu.make_async_copy(out_ref.at[done], out_hbm.at[done], e_sem.at[tile // 2])
+            )
+            results[-1].start()
 
     for kv in range(2):
         keep_own(kv).wait()
@@ -367,6 +389,8 @@
             keep_round(kv, t).wait()
     for i in range(1, 8):
         pltpu.make_async_copy(picked.at[i], picked.at[i], c_send.at[i]).wait()
+    for copy in results:
+        copy.wait()
 
 
 def fused(query_rows, key_rows, value_rows, selection):
@@ -379,11 +403,11 @@
             jax.ShapeDtypeStruct((BLOCK, DH), bf16),
             jax.ShapeDtypeStruct((8, DH), jnp.float32),
             jax.ShapeDtypeStruct((2, BLOCK, DH), bf16),
-            jax.ShapeDtypeStruct((2, 8, 2, 4, 64, DH), bf16),
+            jax.ShapeDtypeStruct((2, 8, 4, 2, 64, DH), bf16),
         ),
         in_specs=[anywhere] * 4,
         out_specs=(
-            pl.BlockSpec(memory_space=pltpu.VMEM),
+            anywhere,
             pl.BlockSpec(memory_space=pltpu.VMEM),
             anywhere,
             anywhere,
@@ -391,12 +415,15 @@
         scratch_shapes=[pltpu.VMEM((8, 64, DH), bf16)] * 16 + [
             pltpu.SMEM((SLOTS, 16), jnp.int32),
             pltpu.VMEM((BLOCK, DH), bf16),
+            pltpu.VMEM((64, 4 * DH), bf16),
+            pltpu.VMEM((64, 4 * DH), bf16),
+            pltpu.VMEM((BLOCK, DH), bf16),
             pltpu.VMEM((8, 8, 2, 64, DH), bf16),
             pltpu.VMEM((2, 4, 512, DH), bf16),
-            pltpu.VMEM((2, 8, 2, 4, 64, DH), bf16),
+            pltpu.VMEM((2, 8, 4, 2, 64, DH), bf16),
             pltpu.VMEM((2, BLOCK, DH), bf16),
             pltpu.VMEM((BLOCK, 2 * DH), jnp.float32),
-            dma((2,)), dma((2, 9)),
+            dma((4,)), dma((2, 9)), dma((4,)),
             dma((2, 4, 2)), dma((8, 2)),
             dma((8,)), dma((8, PARTS)), dma((8,)), dma((8, PARTS)),
             dma((7,)), dma((7,)), dma((8,)), dma((8, 8)),
@@ -457,7 +484,7 @@
             return absorb(own[0, there], own[1, there], col_ids + i * 512 <= row_ids, peak)
 
         def round_part(t, peak):
-            live = jnp.where(col_ids < 256, sel_ref[1, ctx], sel_ref[2, ctx]) >= 0
+            live = jnp.where(col_ids // 64 % 2 == 0, sel_ref[1, ctx], sel_ref[2, ctx]) >= 0
             return absorb(kv[0, t].reshape(512, DH), kv[1, t].reshape(512, DH), live, peak)
 
         peak = jnp.full((size, DH), -1e30, jnp.float32)
@@ -484,7 +511,7 @@
             pltpu.SMEM((SLOTS, 16), jnp.int32),
             pltpu.VMEM((BLOCK, DH), jnp.bfloat16),
             pltpu.VMEM((2, BLOCK, DH), jnp.bfloat16),
-            pltpu.VMEM((2, 8, 2, 4, 64, DH), jnp.bfloat16),
+            pltpu.VMEM((2, 8, 4, 2, 64, DH), jnp.bfloat16),
             pltpu.VMEM((size, 2 * DH), jnp.float32),
             pltpu.SemaphoreType.DMA((4,)),
         ],

time: 93.9 us -> 94 us (level)
  no operation moved by 1% of the time
where the time goes in v6:
time: 94 us; the launch traced here: 93.8 us
  Pallas kernels  93.6 us (100%)
    pallas_call x1, Pallas kernels, fused(): pl.pallas_call(fused_kernel, out_shape=(jax.ShapeDtypeStruct((BLOCK, DH),...  60.4 us
    pallas_call x1, Pallas kernels, attention(): pl.pallas_call(finish_kernel, out_shape=jax.ShapeDtypeStruct(fast.shape,...  33.2 us

profile of v6, /device:TPU:1, one launch (start us, length us, event | category | flops | bytes accessed | tf_op | source)
XLA Modules:
  0.0 93.8 jit_solution(13098772255805615484)
XLA Ops:
  0.0 60.4 %block_attention.1 = (bf16[2048,128]{1,0:T(8,128)(2,1)}, f32[8,128]{1,0:T(8,128)}, bf16[2,2048,128]{2,1,0:T(8,128)(2,1)}, bf16[2,8,4,2,64,128]{5,4,3,2,1,0:T(8,128)(2,1)}) custom-call(s32[3,16]{1,0:T(4,128)} %bitcast.1, bf16[2048,128]{1,0:T(8,128)(2,1)} %q_hbm.3, bf16[64,512]{1,0:T(8,128)(2,1)} %k_hbm.1, bf16[64,512]{1,0:T(8,128)(2,1)} %v_hbm.1), custom_call_target="tpu_custom_call" | custom-call | tf_op jit(solution)/shard_map/block_attention/pallas_call | solution.py:400
  60.4 33.2 %finish.1 = bf16[2048,128]{1,0:T(8,128)(2,1)} custom-call(bf16[2048,128]{1,0:T(8,128)(2,1)} %get-tuple-element.9.fast_ref, f32[8,128]{1,0:T(8,128)} %get-tuple-element.10.bad_ref, s32[3,16]{1,0:T(4,128)} %bitcast.2, bf16[2048,128]{1,0:T(8,128)(2,1)} %q_hbm.3, bf16[2,2048,128]{2,1,0:T(8,128)(2,1)} %get-tuple-element.11.own_hbm, ...), custom_call_target="tpu_custom_call" | custom-call | tf_op jit(solution)/shard_map/finish/pallas_call | solution.py:500
